TPU v7x, 32 devices: a whole 2x2x4 slice. The times are simulated.
32 devices in a mesh: band: 8 (over y, x, core), field: 4 (over z).
Axes of the slice: x: 2, y: 2, z: 4, core: 2. Of those that a mesh axis runs over, the one named last changes fastest.
Arguments:
- fourier: bfloat16 [144, 256, 2, 1024], P('field', 'band'), may hold values from -6 to 6
- row_length: int32 [256], P('band'), may hold values from 20 to 2064, as said below
- wave_order: int32 [512], replicated, may hold values from 0 to 511, each once
- legendre: bfloat16 [512, 1025, 128], P(('band', 'field')), may hold values from -0.375 to 0.375
- vertical: bfloat16 [2, 72, 72], replicated, may hold values from -0.75 to 0.75
Outputs:
- returned: bfloat16 [144, 256, 2, 1024], P('field', 'band')
Inputs may be any that keep to these rules, and one draw needn't show every extreme that they name: row_length[lat] is a multiple of 4 lying 0 to 12 above 20 + 16 * d with d = min(lat, 255 - lat); the two polar rows have length 20 and the two rows beside the equator lie 12 above. `wave_order`: each pair index appears once.
All inputs are finite; a program needn't handle non-finite values.
Results may differ from a plain program's by a relative error of at most 0.0049.
Values may be sent and summed in bfloat16 or wider, within the bound.
A program may use at most 128 MiB of HBM per device.

v0:
```python
import jax
import jax.numpy as jnp
from jax import lax
from jax.sharding import PartitionSpec as P


def row_parity(total_rows, first_wave):
    row_ids = lax.iota(jnp.int32, total_rows)
    boundary = total_rows - 1 - first_wave
    degree = jnp.where(row_ids < boundary, row_ids, row_ids - boundary)
    parity = (1 - 2 * (degree % 2)).astype(jnp.float32)
    return (row_ids, boundary, parity)


def direct_pair(inputs):
    values, table_pair, first_wave = inputs
    total_rows = table_pair.shape[0]
    lat_half = table_pair.shape[1]
    row_ids, boundary, parity = row_parity(total_rows, first_wave)
    northern = values[:, :, :lat_half]
    southern = jnp.flip(values[:, :, lat_half:], axis=2)
    stacked = jnp.stack([northern, southern])
    partial_sums = jnp.einsum(
        "hscl,rl->hscr", stacked, table_pair, preferred_element_type=jnp.float32
    )
    combined = partial_sums[0] + parity * partial_sums[1]
    owner_mask = jnp.stack([row_ids < boundary, row_ids >= boundary])
    return jnp.where(owner_mask[:, None, :], combined, 0.0).astype(jnp.bfloat16)


def inverse_pair(inputs):
    updated, table_pair, first_wave = inputs
    total_rows = table_pair.shape[0]
    row_ids, boundary, parity = row_parity(total_rows, first_wave)
    flipped = updated * parity.astype(jnp.bfloat16)
    stacked = jnp.stack([updated, flipped])
    halves = jnp.einsum("hscr,rl->hscl", stacked, table_pair, preferred_element_type=jnp.float32)
    joined = jnp.concatenate([halves[0], jnp.flip(halves[1], axis=2)], axis=2)
    return joined.astype(jnp.bfloat16)


def mix_levels(spectral, vertical):
    levels = vertical.shape[1]
    shaped = spectral.reshape(spectral.shape[0], 2, 2, levels, 2, spectral.shape[4])
    mixed_levels = jnp.einsum(
        "qab,psqbcr->psqacr", vertical, shaped, preferred_element_type=jnp.float32
    )
    return mixed_levels.astype(jnp.bfloat16).reshape(spectral.shape)


def transform_held(arrived_data, legendre, pair_first, vertical):
    pairs_held = legendre.shape[0]
    field_levels = arrived_data.shape[1]
    lat_total = arrived_data.shape[3]
    values = arrived_data.reshape(pairs_held, 2, field_levels * 2, lat_total)

    def complete(inputs):
        values_pair, table_pair, first_wave = inputs
        spectral = direct_pair((values_pair, table_pair, first_wave))
        shaped = spectral.reshape(1, 2, field_levels, 2, spectral.shape[2])
        updated = mix_levels(shaped, vertical).reshape(spectral.shape)
        return inverse_pair((updated, table_pair, first_wave))

    grid_part = lax.map(complete, (values, legendre, pair_first))
    return grid_part.reshape(pairs_held * 2, field_levels, 2, lat_total)


def per_device(fourier, row_length, wave_order, legendre, vertical):
    wave_total = fourier.shape[3]
    field_count = lax.axis_size("field")
    band_index = lax.axis_index("band")
    field_index = lax.axis_index("field")
    pairs_held = legendre.shape[0]
    wave_ids = lax.iota(jnp.int32, wave_total)
    wave_count = jnp.minimum(wave_total, row_length // 2)
    in_range = wave_ids[None, :] < wave_count[:, None]
    nothing = jnp.zeros((), jnp.bfloat16)
    masked_input = jnp.where(in_range[None, :, None, :], fourier, nothing)
    ordering = jnp.stack([wave_order, wave_total - 1 - wave_order], axis=1).reshape(wave_total)
    outgoing = jnp.take(masked_input, ordering, axis=3).transpose(3, 0, 2, 1)
    start_pair = (band_index * field_count + field_index) * pairs_held
    pair_first = lax.dynamic_slice_in_dim(wave_order, start_pair, pairs_held)
    band_data = lax.all_to_all(outgoing, "band", split_axis=0, concat_axis=3, tiled=True)
    arrived_data = lax.all_to_all(band_data, "field", split_axis=0, concat_axis=1, tiled=True)
    grid_part = transform_held(arrived_data, legendre, pair_first, vertical)
    band_part = lax.all_to_all(grid_part, "field", split_axis=1, concat_axis=0, tiled=True)
    sorted_back = lax.all_to_all(band_part, "band", split_axis=3, concat_axis=0, tiled=True)
    position = jnp.zeros((wave_total,), jnp.int32).at[ordering].set(wave_ids)
    restored = jnp.take(sorted_back, position, axis=0).transpose(1, 3, 2, 0)
    return jnp.where(in_range[None, :, None, :], restored, nothing)


def solution(mesh):
    placed = (P("field", "band", None, None), P("band"), P(), P(("band", "field"), None, None), P())
    return jax.shard_map(
        per_device,
        mesh=mesh,
        in_specs=placed,
        out_specs=P("field", "band", None, None),
        check_vma=False,
    )
```

profile of v0, /device:TPU:11, one launch (start us, length us, event | category | flops | bytes accessed | tf_op | source)
XLA Modules:
  0.0 1039.2 jit_solution(11936836815070865883)
XLA Ops:
  2.7 26.7 %copy.49 = bf16[36,32,2,1024]{0,1,2,3:T(8,128)(2,1)} copy(bf16[36,32,2,1024]{3,2,1,0:T(2,128)(2,1)} %param.7) | data formatting | bytes 9437184 | tf_op args[0]
  29.4 11.9 %broadcast_select_fusion = bf16[36,32,2,1024]{0,1,2,3:T(8,128)(2,1)} fusion(bf16[36,32,2,1024]{0,1,2,3:T(8,128)(2,1)} %copy.49, pred[32,1024]{0,1:T(8,128)(4,1)S(1)} %iota_compare_fusion.3), kind=kLoop, calls=%fused_computation.51 | loop fusion | flops 2359296 | bytes 9469952 | tf_op jit(solution)/shard_map/jit(_where)/select_n | solution.py:78
  41.3 19.2 %gather_fusion = bf16[1024,36,32,2]{1,2,3,0:T(8,128)(2,1)} fusion(bf16[36,32,2,1024]{0,1,2,3:T(8,128)(2,1)} %broadcast_select_fusion, s32[1024]{0:T(1024)S(1)} %broadcast_clamp_fusion), kind=kCustom, calls=%fused_computation | custom fusion | bytes 9441280 | tf_op jit(solution)/shard_map/jit(_take)/gather | solution.py:80
  60.5 14.9 %fusion.37 = bf16[1024,2,32,36]{3,2,1,0:T(8,128)(2,1)} fusion(bf16[1024,36,32,2]{1,2,3,0:T(8,128)(2,1)} %gather_fusion, pred[1024]{0:T(1024)(128)(4,1)S(1)} %compare_and_fusion), kind=kLoop, calls=%fused_computation.72 | loop fusion | flops 2359296 | bytes 9438208
  75.4 43.8 %reshape.208 = bf16[8,2,147456]{2,1,0:T(2,128)(2,1)} reshape(bf16[1024,2,32,36]{3,2,1,0:T(8,128)(2,1)} %fusion.37) | data formatting | bytes 9437184
  119.2 58.9 %all_to_all.69 = bf16[8,2,147456]{2,1,0:T(2,128)(2,1)} all-to-all(bf16[8,2,147456]{2,1,0:T(2,128)(2,1)} %reshape.208), channel_id=1, replica_groups=mesh['band'=8,'field'=4] {'band'}, dimensions={0} | all-to-all | bytes 9437184 | tf_op jit(solution)/shard_map/all_to_all | solution.py:83
  178.1 47.7 %reshape.209 = bf16[1024,2,32,36]{3,2,1,0:T(8,128)(2,1)} reshape(bf16[8,2,147456]{2,1,0:T(2,128)(2,1)} %all_to_all.69) | data formatting | bytes 9437184
  225.7 24.9 %copy.50 = bf16[8,128,36,2,32]{1,4,0,3,2:T(8,128)(2,1)} copy(bf16[8,128,36,2,32]{2,4,3,1,0:T(8,128)(2,1)} %bitcast.85) | data formatting | bytes 9437184 | tf_op jit(solution)/shard_map/all_to_all | solution.py:83
  250.7 12.5 %copy.51 = bf16[128,36,2,256]{3,2,1,0:T(2,128)(2,1)} copy(bf16[128,36,2,256]{0,3,2,1:T(8,128)(2,1)} %bitcast.89) | data formatting | bytes 9437184 | tf_op jit(solution)/shard_map/all_to_all | solution.py:83
  263.1 5.1 all-to-all-start.1
  269.0 5.2 copy.54
  274.3 94.7 %all-to-all-done.1 = bf16[128,36,2,256]{3,2,1,0:T(2,128)(2,1)} async-done(((bf16[128,36,2,256]{3,2,1,0:T(2,128)(2,1)}), bf16[128,36,2,256]{3,2,1,0:T(2,128)(2,1)}, u32[]{:S(2)}, u32[]{:S(2)}) %all-to-all-start.1) | async-done | bytes 4718624 | tf_op jit(solution)/shard_map/all_to_all | solution.py:84
  369.0 5.8 copy.52
  374.8 9.4 copy.53
  384.3 8.1 reshape.176
  392.3 356.3 %while.12 = (s32[]{:T(128)}, bf16[16,2,288,256]{3,2,1,0:T(8,128)(2,1)}, s32[16]{0:T(128)S(1)}, bf16[16,2,288,256]{3,2,1,0:T(8,128)(2,1)}, bf16[16,1025,128]{2,1,...) while((s32[]{:T(128)}, bf16[16,2,288,256]{3,2,1,0:T(8,128)(2,1)}, ...), condition=%wide.region_2.3_spmd, body=%wide.region_1.2_spmd.sunk | while | flops 695070208 | bytes 41895816 | solution.py:64
  402.2 4.4 squeeze.35
  424.4 4.4 squeeze.35
  446.7 4.4 squeeze.35
  647.0 4.4 squeeze.35
  669.2 4.4 squeeze.35
  748.6 8.0 reshape.205
  756.7 7.5 copy.64
  764.1 107.9 %all_to_all.70 = bf16[32,144,2,256]{3,0,2,1:T(8,128)(2,1)S(1)} all-to-all(bf16[32,144,2,256]{3,0,2,1:T(8,128)(2,1)S(1)} %copy.64), channel_id=1, replica_groups=mesh['band'=8,'field'=4] {'field'}, dimensions={1} | all-to-all | bytes 9437184 | tf_op jit(solution)/shard_map/all_to_all | solution.py:86
  874.8 12.5 %copy.57 = bf16[128,36,2,256]{0,2,1,3:T(2,128)(2,1)} copy(bf16[128,36,2,256]{3,0,2,1:T(8,128)(2,1)} %bitcast.88) | data formatting | bytes 9437184 | tf_op jit(solution)/shard_map/all_to_all | solution.py:86
  887.3 7.0 all-to-all-start.3
  898.6 48.9 %all-to-all-done.3 = bf16[128,36,2,256]{0,2,1,3:T(2,128)(2,1)} async-done(((bf16[128,36,2,256]{0,2,1,3:T(2,128)(2,1)}), bf16[128,36,2,256]{0,2,1,3:T(2,128)(2,1)}, u32[]{:S(2)}, u32[]{:S(2)}) %all-to-all-start.3) | async-done | bytes 4718624 | tf_op jit(solution)/shard_map/all_to_all | solution.py:87
  947.5 5.7 copy.58
  953.2 26.4 %copy.65 = bf16[8,128,36,2,32]{2,4,3,1,0:T(8,128)(2,1)} copy(bf16[8,128,36,2,32]{1,4,0,3,2:T(8,128)(2,1)} %bitcast.90) | data formatting | bytes 9437184 | tf_op jit(solution)/shard_map/all_to_all | solution.py:87
  979.7 19.2 %gather_fusion.1 = bf16[1024,36,2,32]{1,3,2,0:T(8,128)(2,1)} fusion(bf16[1024,36,2,32]{1,3,2,0:T(8,128)(2,1)} %bitcast.84, s32[1024]{0:T(1024)S(1)} %fusion.30), kind=kCustom, calls=%fused_computation.1 | custom fusion | bytes 9441280 | tf_op jit(solution)/shard_map/jit(_take)/gather | solution.py:89
  998.9 12.3 %bitcast_select_fusion = bf16[36,32,2,1024]{0,1,2,3:T(8,128)(2,1)} fusion(bf16[1024,36,2,32]{1,3,2,0:T(8,128)(2,1)} %gather_fusion.1, pred[1024]{0:T(1024)(128)(4,1)S(1)} %compare_and_fusion.1, pred[32,1024]{0,1:T(8,128)(4,1)S(1)} %copy-done.1), kind=kLoop, calls=%fused_computation.49 | loop fusion | flops 4718592 | bytes 9470976 | tf_op jit(solution)/shard_map/jit(_where)/select_n | solution.py:90
  1011.2 27.7 %copy.61 = bf16[36,32,2,1024]{3,2,1,0:T(2,128)(2,1)} copy(bf16[36,32,2,1024]{0,1,2,3:T(8,128)(2,1)} %bitcast_select_fusion) | data formatting | bytes 9437184 | tf_op jit(solution)/shard_map/jit(_where)/select_n | solution.py:90
  (306 shorter events, 334.0 us)
Async XLA Ops:
  2.7 26.7 %copy-start = (pred[32,1024]{0,1:T(8,128)(4,1)}, pred[32,1024]{0,1:T(8,128)(4,1)S(1)}, u32[]{:S(2)}) copy-start(pred[32,1024]{0,1:T(8,128)(4,1)S(1)} %iota_compare_fusion.3) | copy-start | bytes 98308
  263.1 105.9 %all-to-all-start.1 = ((bf16[128,36,2,256]{3,2,1,0:T(2,128)(2,1)}), bf16[128,36,2,256]{3,2,1,0:T(2,128)(2,1)}, u32[]{:S(2)}, u32[]{:S(2)}) async-start(bf16[128,36,2,256]{3,2,1,0:T(2,128)(2,1)} %copy.51), calls=%async_computation.1 | async-start | bytes 9437184 | tf_op jit(solution)/shard_map/all_to_all | solution.py:84
  384.3 8.1 copy-start.2
  887.3 60.3 %all-to-all-start.3 = ((bf16[128,36,2,256]{0,2,1,3:T(2,128)(2,1)}), bf16[128,36,2,256]{0,2,1,3:T(2,128)(2,1)}, u32[]{:S(2)}, u32[]{:S(2)}) async-start(bf16[128,36,2,256]{0,2,1,3:T(2,128)(2,1)} %copy.57), calls=%async_computation.3 | async-start | bytes 9437184 | tf_op jit(solution)/shard_map/all_to_all | solution.py:87
  979.7 19.2 %copy-start.1 = (pred[32,1024]{0,1:T(8,128)(4,1)S(1)}, pred[32,1024]{0,1:T(8,128)(4,1)}, u32[]{:S(2)}) copy-start(pred[32,1024]{0,1:T(8,128)(4,1)} %copy-done) | copy-start | bytes 98308
where the time goes:
time: 1060 us; the launch traced here: 1040 us
  local copies, waits for them, and re-layouts  553 us (52%)
  blocking collectives  167 us (16%)
  waiting for transfers between devices  144 us (14%)
  matrix products  94.6 us (9%)
  other arithmetic  58.6 us (6%)
  starting transfers between devices  12.1 us (1%)
  loops' own time  10.6 us (1%)
    squeeze x32, local copies, waits for them, and re-layouts, direct_pair(): combined = partial_sums[0] + parity * partial_sums[1]  123 us
    unnamed x9, local copies, waits for them, and re-layouts  118 us
    all_to_all x1, blocking collectives, per_device(): lax.all_to_all(grid_part, 'field', split_axis=1, concat_axis=0, tiled=True)  108 us
    all_to_all x1, waiting for transfers between devices, per_device(): lax.all_to_all(band_data, 'field', split_axis=0, concat_axis=1, tiled=True)  94.7 us
    all_to_all x1, blocking collectives, per_device(): lax.all_to_all(outgoing, 'band', split_axis=0, concat_axis=3, tiled=True)  58.9 us
    all_to_all x1, waiting for transfers between devices, per_device(): lax.all_to_all(band_part, 'band', split_axis=3, concat_axis=0, tiled=True)  48.9 us
    slice x16, local copies, waits for them, and re-layouts, direct_pair(): combined = partial_sums[0] + parity * partial_sums[1]  43.8 us
    all_to_all x2, local copies, waits for them, and re-layouts, per_device(): lax.all_to_all(outgoing, 'band', split_axis=0, concat_axis=3, tiled=True)  37.4 us
  transfers between devices with their start and end apart: 2, of which 2 were waited for; matrix products, arithmetic and copies ran while one was open for 1% of the time, Pallas kernels for 0%

commit v1 on v0

v1 whole, which is shorter than its diff:
```python
import functools

import jax
import jax.numpy as jnp
from jax import lax
from jax.experimental import pallas as pl
from jax.experimental.pallas import tpu as pltpu
from jax.sharding import PartitionSpec as P

MESH = pl.DeviceIdType.MESH


def exchange_kernel(bands, fields, src, dst, send_sem, recv_sem, own_sem):
    total = bands * fields
    band, field = lax.axis_index("band"), lax.axis_index("field")
    me = band * fields + field

    def other(step):
        peer = lax.rem(me + step, total)
        return peer, (peer // fields, lax.rem(peer, fields))

    barrier = pltpu.get_barrier_semaphore()

    @pl.loop(1, total)
    def _(step):
        _, where = other(step)
        pl.semaphore_signal(barrier, inc=1, device_id=where, device_id_type=MESH)

    own = pltpu.make_async_copy(src.at[me], dst.at[me], own_sem)
    own.start()
    pl.semaphore_wait(barrier, total - 1)

    def copy(step):
        peer, where = other(step)
        return pltpu.make_async_remote_copy(
            src_ref=src.at[peer],
            dst_ref=dst.at[me],
            send_sem=send_sem.at[step],
            recv_sem=recv_sem.at[step],
            device_id=where,
            device_id_type=MESH,
        )

    @pl.loop(1, total)
    def _(step):
        copy(step).start()

    @pl.loop(1, total)
    def _(step):
        copy(step).wait_send()
        peer = lax.rem(me + total - step, total)
        pltpu.make_async_remote_copy(
            src_ref=src.at[peer],
            dst_ref=dst.at[peer],
            send_sem=send_sem.at[step],
            recv_sem=recv_sem.at[step],
            device_id=(peer // fields, lax.rem(peer, fields)),
            device_id_type=MESH,
        ).wait_recv()

    own.wait()


def exchange(data, bands, fields, ident):
    total = bands * fields
    return pl.pallas_call(
        functools.partial(exchange_kernel, bands, fields),
        out_shape=jax.ShapeDtypeStruct(data.shape, data.dtype),
        in_specs=[pl.BlockSpec(memory_space=pl.ANY)],
        out_specs=pl.BlockSpec(memory_space=pl.ANY),
        scratch_shapes=[
            pltpu.SemaphoreType.DMA((total,)),
            pltpu.SemaphoreType.DMA((total,)),
            pltpu.SemaphoreType.DMA,
        ],
        compiler_params=pltpu.CompilerParams(collective_id=ident, has_side_effects=True),
    )(data)


def pair_kernel(waves, first, x_ref, table_ref, mix_ref, out_ref):
    table = table_ref[0]
    rows, half = table.shape
    boundary = waves - first[pl.program_id(0)]
    up = lax.broadcasted_iota(jnp.int32, (half, half), 0)
    across = lax.broadcasted_iota(jnp.int32, (half, half), 1)
    turn = (up + across == half - 1).astype(jnp.float32).astype(jnp.bfloat16)
    southern = jnp.dot(table, turn, preferred_element_type=jnp.float32)
    northern = table.astype(jnp.float32)
    row_ids = lax.broadcasted_iota(jnp.int32, (rows, half), 0)
    held = row_ids < boundary
    degree = jnp.where(held, row_ids, row_ids - boundary)
    southern = jnp.where(degree % 2 == 0, southern, -southern)
    zero = jnp.zeros((), jnp.float32)
    full = jnp.concatenate(
        [
            jnp.where(held, northern, zero).astype(jnp.bfloat16),
            jnp.where(held, southern, zero).astype(jnp.bfloat16),
            jnp.where(held, zero, northern).astype(jnp.bfloat16),
            jnp.where(held, zero, southern).astype(jnp.bfloat16),
        ],
        axis=1,
    )
    spectral = lax.dot_general(
        x_ref[0], full, (((1,), (1,)), ((), ())), preferred_element_type=jnp.float32
    ).astype(jnp.bfloat16)
    updated = jnp.dot(mix_ref[...], spectral, preferred_element_type=jnp.float32).astype(jnp.bfloat16)
    out_ref[0] = jnp.dot(updated, full, preferred_element_type=jnp.float32).astype(jnp.bfloat16)


def transform(values, legendre, mixing, pair_first, waves):
    pairs, columns, span = values.shape
    rows, half = legendre.shape[1:]
    flops = 2 * pairs * columns * rows * (2 * span + columns)
    return pl.pallas_call(
        functools.partial(pair_kernel, waves),
        grid_spec=pltpu.PrefetchScalarGridSpec(
            num_scalar_prefetch=1,
            grid=(pairs,),
            in_specs=[
                pl.BlockSpec((1, columns, span), lambda k, first: (k, 0, 0)),
                pl.BlockSpec((1, rows, half), lambda k, first: (k, 0, 0)),
                pl.BlockSpec((columns, columns), lambda k, first: (0, 0)),
            ],
            out_specs=pl.BlockSpec((1, columns, span), lambda k, first: (k, 0, 0)),
        ),
        out_shape=jax.ShapeDtypeStruct(values.shape, jnp.bfloat16),
        compiler_params=pltpu.CompilerParams(vmem_limit_bytes=48 * 1024 * 1024),
        cost_estimate=pl.CostEstimate(
            flops=flops, bytes_accessed=4 * values.size + 2 * legendre.size, transcendentals=0
        ),
    )(pair_first, values, legendre, mixing)


def mixing_matrix(vertical, fields):
    levels = vertical.shape[1]
    total = 2 * levels
    blocks = jnp.zeros((2, levels, 2, levels), vertical.dtype)
    blocks = blocks.at[0, :, 0, :].set(vertical[0]).at[1, :, 1, :].set(vertical[1])
    block = blocks.reshape(fields, total // fields, fields, total // fields)
    parts = jnp.eye(2, dtype=vertical.dtype)
    return jnp.einsum("zfyg,cd->zcfydg", block, parts).reshape(2 * total, 2 * total)


def per_device(fourier, row_length, wave_order, legendre, vertical):
    levels, lats, _, waves = fourier.shape
    bands, fields = lax.axis_size("band"), lax.axis_size("field")
    total = bands * fields
    pairs = legendre.shape[0]
    wave_ids = lax.iota(jnp.int32, waves)
    wave_count = jnp.minimum(waves, row_length // 2)
    in_range = wave_ids[None, :] < wave_count[:, None]
    nothing = jnp.zeros((), jnp.bfloat16)
    masked = jnp.where(in_range[None, :, None, :], fourier, nothing)
    ordering = jnp.stack([wave_order, waves - 1 - wave_order], axis=1).reshape(waves)
    choose = (ordering[:, None] == wave_ids[None, :]).astype(jnp.bfloat16)
    start_pair = (lax.axis_index("band") * fields + lax.axis_index("field")) * pairs
    pair_first = lax.dynamic_slice_in_dim(wave_order, start_pair, pairs)

    flat = masked.transpose(2, 0, 1, 3).reshape(2 * levels * lats, waves)
    outgoing = lax.dot_general(
        choose, flat, (((1,), (1,)), ((), ())), preferred_element_type=jnp.float32
    ).astype(jnp.bfloat16)
    arrived = exchange(outgoing.reshape(total, 2 * pairs, 2 * levels * lats), bands, fields, 0)
    values = arrived.reshape(bands, fields, pairs, 2, 2 * levels, lats).transpose(2, 1, 4, 3, 0, 5)
    values = values.reshape(pairs, fields * 2 * levels, 2 * bands * lats)
    grid_part = transform(values, legendre, mixing_matrix(vertical, fields), pair_first, waves)
    back = grid_part.reshape(pairs, fields, 2 * levels, 2, bands, lats).transpose(4, 1, 0, 3, 2, 5)
    home = exchange(back.reshape(total, 2 * pairs, 2 * levels * lats), bands, fields, 1)
    restored = lax.dot_general(
        home.reshape(waves, 2 * levels * lats), choose, (((0,), (0,)), ((), ())),
        preferred_element_type=jnp.float32,
    ).astype(jnp.bfloat16)
    restored = restored.reshape(2, levels, lats, waves).transpose(1, 2, 0, 3)
    return jnp.where(in_range[None, :, None, :], restored, nothing)


def solution(mesh):
    placed = (P("field", "band", None, None), P("band"), P(), P(("band", "field"), None, None), P())
    return jax.shard_map(
        per_device,
        mesh=mesh,
        in_specs=placed,
        out_specs=P("field", "band", None, None),
        check_vma=False,
    )
```

time: 1060 us -> 433 us (0.41); the launches traced: 1040 us -> 428 us
  local copies, waits for them, and re-layouts: 553 us -> 147 us
  Pallas kernels: 0 us -> 243 us
  blocking collectives: 167 us -> 0 us
  waiting for transfers between devices: 144 us -> 0 us
  matrix products: 94.6 us -> 18.9 us
  other arithmetic: 58.6 us -> 18.6 us
  starting transfers between devices: 12.1 us -> 0 us
  loops' own time: 10.6 us -> 0 us
    pallas_call x0 -> x3, Pallas kernels: none -> 243 us  [the longest x2 214 us: exchange(): pl.pallas_call(functools.partial(exchange_kernel, bands, fields), out_sha...]
    all_to_all x2 -> x0, blocking collectives: 167 us -> none  [the longest x1 108 us: per_device(): lax.all_to_all(grid_part, 'field', split_axis=1, concat_axis=0, tiled=True)]
    all_to_all x2 -> x0, waiting for transfers between devices: 144 us -> none  [the longest x1 94.7 us: per_device(): lax.all_to_all(band_data, 'field', split_axis=0, concat_axis=1, tiled=True)]
    squeeze x48 -> x0, local copies, waits for them, and re-layouts: 139 us -> none  [the longest x32 123 us: direct_pair(): combined = partial_sums[0] + parity * partial_sums[1]]
    unnamed x9 -> x7, local copies, waits for them, and re-layouts: 118 us -> 7.43 us
    all_to_all x8 -> x0, local copies, waits for them, and re-layouts: 100 us -> none  [the longest x2 37.4 us: per_device(): lax.all_to_all(outgoing, 'band', split_axis=0, concat_axis=3, tiled=True)]
    dot_general x48 -> x2, matrix products: 94.6 us -> 18.9 us  [the longest x1 9.6 us: per_device(): lax.dot_general(home.reshape(waves, 2 * levels * lats), choose, (((0,), (...]
    reshape x5 -> x7, local copies, waits for them, and re-layouts: 23.9 us -> 81.5 us  [the longest x1 21.7 us: per_device(): back.reshape(total, 2 * pairs, 2 * levels * lats)]
  transfers between devices with their start and end apart: 2 -> 0, of which waited for: 2 -> 0; matrix products, arithmetic and copies ran while one was open for 1% -> 0% of each run, Pallas kernels for 0% -> 0%
where the time goes in v1:
time: 433 us; the launch traced here: 428 us
  Pallas kernels  243 us (56%)
  local copies, waits for them, and re-layouts  147 us (34%)
  matrix products  18.9 us (4%)
  other arithmetic  18.6 us (4%)
    pallas_call x2, Pallas kernels, exchange(): pl.pallas_call(functools.partial(exchange_kernel, bands, fields), out_sha...  214 us
    pallas_call x1, Pallas kernels, transform(): pl.pallas_call(functools.partial(pair_kernel, waves), grid_spec=pltpu.Pre...  28.8 us
    transpose x1, local copies, waits for them, and re-layouts, per_device(): arrived.reshape(bands, fields, pairs, 2, 2 * levels, lats)  24.4 us
    transpose x1, local copies, waits for them, and re-layouts, per_device(): grid_part.reshape(pairs, fields, 2 * levels, 2, bands, lats)  24.3 us
    reshape x1, local copies, waits for them, and re-layouts, per_device(): back.reshape(total, 2 * pairs, 2 * levels * lats)  21.7 us
    reshape x1, local copies, waits for them, and re-layouts, per_device(): arrived.reshape(bands, fields, pairs, 2, 2 * levels, lats)  21.7 us
    reshape x2, local copies, waits for them, and re-layouts, per_device(): values = values.reshape(pairs, fields * 2 * levels, 2 * bands * lats)  21.6 us
    reshape x1, local copies, waits for them, and re-layouts, per_device(): grid_part.reshape(pairs, fields, 2 * levels, 2, bands, lats)  16 us

profile of v1, /device:TPU:11, one launch (start us, length us, event | category | flops | bytes accessed | tf_op | source)
XLA Modules:
  0.0 427.6 jit_solution(6986646156582864040)
XLA Ops:
  0.0 0.8 dynamic_slice.3.first
  0.8 0.7 fusion.3
  1.4 0.1 iota_compare_fusion.3
  1.5 0.0 copy-start.2
  1.5 6.4 %copy_select_fusion = bf16[36,32,2,1024]{3,1,0,2:T(8,128)(2,1)} fusion(bf16[36,32,2,1024]{3,2,1,0:T(2,128)(2,1)} %param.9, pred[32,1024]{1,0:T(8,128)(4,1)S(1)} %iota_compare_fusion.3), kind=kLoop, calls=%fused_computation.4 | loop fusion | flops 2359296 | bytes 9469952 | tf_op jit(solution)/shard_map/jit(_where)/select_n | solution.py:153
  7.9 0.0 copy-done.2
  7.9 0.1 copy.10
  8.1 0.2 eq.18
  8.2 9.3 %convolution_convert_fusion.1 = bf16[1024,2304]{1,0:T(8,128)(2,1)} fusion(bf16[2304,1024]{1,0:T(8,128)(2,1)} %bitcast.28, s32[1024]{0:T(1024)S(1)} %eq.18), kind=kOutput, calls=%fused_computation.2 | convolution fusion | flops 4835246080 | bytes 9441280 | tf_op jit(solution)/shard_map/dot_general | solution.py:160
  17.5 107.8 %shard_map.55 = bf16[32,32,2304]{2,1,0:T(8,128)(2,1)} custom-call(bf16[32,32,2304]{2,1,0:T(8,128)(2,1)} %bitcast.31), custom_call_target="tpu_custom_call" | custom-call | tf_op jit(solution)/shard_map/pallas_call | solution.py:66
  125.3 21.7 %reshape.131 = bf16[8,4,16,2,72,32]{5,4,3,2,1,0:T(8,128)(2,1)} reshape(bf16[32,32,2304]{2,1,0:T(8,128)(2,1)} %shard_map.55) | data formatting | bytes 9437184 | tf_op jit(solution)/shard_map/reshape | solution.py:164
  146.9 24.4 %copy.12 = bf16[16,4,72,2,8,32]{2,1,5,4,3,0:T(4,128)(2,1)} copy(bf16[16,4,72,2,8,32]{5,2,3,0,1,4:T(8,128)(2,1)} %bitcast.26) | data formatting | bytes 9437184 | tf_op jit(solution)/shard_map/transpose | solution.py:164
  171.4 13.7 %reshape.132 = bf16[16,288,512]{1,2,0:T(8,128)(2,1)} reshape(bf16[16,4,72,2,8,32]{2,1,5,4,3,0:T(4,128)(2,1)} %copy.12) | data formatting | bytes 9437184 | tf_op jit(solution)/shard_map/reshape | solution.py:165
  185.1 7.9 %copy.14.x_ref = bf16[16,288,512]{2,1,0:T(8,128)(2,1)} copy(bf16[16,288,512]{1,2,0:T(8,128)(2,1)} %reshape.132) | data formatting | bytes 9437184 | tf_op jit(solution)/shard_map/reshape | solution.py:165
  193.0 0.0 copy-start.1
  193.0 5.2 %copy.15.table_ref = bf16[16,1025,128]{2,1,0:T(8,128)(2,1)} copy(bf16[16,1025,128]{2,0,1:T(8,128)(2,1)} %param.12) | data formatting | bytes 8396800 | tf_op args[3]
  198.2 0.0 copy-done.1
  198.3 0.1 copy.13
  198.3 0.1 reshape.135
  198.4 0.6 multiply_bitcast_fusion
  199.0 0.4 reshape.136.mix_ref
  199.4 0.0 copy-start
  199.4 2.2 copy-done
  201.6 28.8 %shard_map.56 = bf16[16,288,512]{2,1,0:T(8,128)(2,1)} custom-call(s32[16]{0:T(128)S(1)} %dynamic_slice.3.first, bf16[16,288,512]{2,1,0:T(8,128)(2,1)} %copy.14.x_ref, bf16[16,1025,128]{2,1,0:T(8,128)(2,1)S(1)} %copy-done, bf16[288,288]{1,0:T(8,128)(2,1)S(1)} %reshape.136.mix_ref), custom_call_target="tpu_custom_call" | custom-call | flops 12393676800 | bytes 13635584 | tf_op jit(solution)/shard_map/pallas_call | solution.py:114
  230.5 8.0 %copy.16 = bf16[16,288,512]{1,2,0:T(8,128)(2,1)} copy(bf16[16,288,512]{2,1,0:T(8,128)(2,1)} %shard_map.56) | data formatting | bytes 9437184 | tf_op jit(solution)/shard_map/pallas_call | solution.py:114
  238.4 16.0 %reshape.137 = bf16[16,4,72,2,8,32]{2,1,5,4,3,0:T(4,128)(2,1)} reshape(bf16[16,288,512]{1,2,0:T(8,128)(2,1)} %copy.16) | data formatting | bytes 9437184 | tf_op jit(solution)/shard_map/reshape | solution.py:167
  254.4 24.3 %copy.17 = bf16[8,4,16,2,72,32]{5,4,3,2,1,0:T(8,128)(2,1)} copy(bf16[8,4,16,2,72,32]{4,1,5,0,3,2:T(4,128)(2,1)} %bitcast.27) | data formatting | bytes 9437184 | tf_op jit(solution)/shard_map/transpose | solution.py:167
  278.7 21.7 %reshape.138.src = bf16[32,32,2304]{2,1,0:T(8,128)(2,1)} reshape(bf16[8,4,16,2,72,32]{5,4,3,2,1,0:T(8,128)(2,1)} %copy.17) | data formatting | bytes 9437184 | tf_op jit(solution)/shard_map/reshape | solution.py:168
  300.4 106.7 %shard_map.57 = bf16[32,32,2304]{2,1,0:T(8,128)(2,1)} custom-call(bf16[32,32,2304]{2,1,0:T(8,128)(2,1)} %reshape.138.src), custom_call_target="tpu_custom_call" | custom-call | tf_op jit(solution)/shard_map/pallas_call | solution.py:66
  407.1 9.6 %convolution_convert_fusion = bf16[2304,1024]{1,0:T(8,128)(2,1)} fusion(bf16[1024,2304]{1,0:T(8,128)(2,1)} %bitcast.30, s32[1024]{0:T(1024)S(1)} %eq.18), kind=kOutput, calls=%fused_computation.1 | convolution fusion | flops 4835246080 | bytes 9441280 | tf_op jit(solution)/shard_map/dot_general | solution.py:169
  416.7 10.9 %fusion = bf16[36,32,2,1024]{3,2,1,0:T(2,128)(2,1)} fusion(pred[32,1024]{1,0:T(8,128)(4,1)S(1)} %iota_compare_fusion.3, bf16[2,36,32,1024]{3,2,1,0:T(8,128)(2,1)} %bitcast.29), kind=kLoop, calls=%fused_computation.3 | loop fusion | flops 2359296 | bytes 9469952 | tf_op jit(solution)/shard_map/jit(_where)/select_n | solution.py:174
  (6 shorter events, 0.0 us)
Async XLA Ops:
  1.5 6.4 %copy-start.2 = (s32[512]{0:T(512)S(1)}, s32[512]{0:T(512)}, u32[]{:S(2)}) copy-start(s32[512]{0:T(512)} %param.11) | copy-start | bytes 6148
  193.0 5.2 %copy-start.1 = (bf16[2,72,72]{2,1,0:T(8,128)(2,1)S(1)}, bf16[2,72,72]{2,1,0:T(8,128)(2,1)}, u32[]{:S(2)}) copy-start(bf16[2,72,72]{2,1,0:T(8,128)(2,1)} %param.13) | copy-start | bytes 62212
  199.4 2.2 copy-start

commit v2 on v1

--- a/solution.py
+++ b/solution.py
@@ -78,33 +78,8 @@
 
 
 def pair_kernel(waves, first, x_ref, table_ref, mix_ref, out_ref):
-    table = table_ref[0]
-    rows, half = table.shape
-    boundary = waves - first[pl.program_id(0)]
-    up = lax.broadcasted_iota(jnp.int32, (half, half), 0)
-    across = lax.broadcasted_iota(jnp.int32, (half, half), 1)
-    turn = (up + across == half - 1).astype(jnp.float32).astype(jnp.bfloat16)
-    southern = jnp.dot(table, turn, preferred_element_type=jnp.float32)
-    northern = table.astype(jnp.float32)
-    row_ids = lax.broadcasted_iota(jnp.int32, (rows, half), 0)
-    held = row_ids < boundary
-    degree = jnp.where(held, row_ids, row_ids - boundary)
-    southern = jnp.where(degree % 2 == 0, southern, -southern)
-    zero = jnp.zeros((), jnp.float32)
-    full = jnp.concatenate(
-        [
-            jnp.where(held, northern, zero).astype(jnp.bfloat16),
-            jnp.where(held, southern, zero).astype(jnp.bfloat16),
-            jnp.where(held, zero, northern).astype(jnp.bfloat16),
-            jnp.where(held, zero, southern).astype(jnp.bfloat16),
-        ],
-        axis=1,
-    )
-    spectral = lax.dot_general(
-        x_ref[0], full, (((1,), (1,)), ((), ())), preferred_element_type=jnp.float32
-    ).astype(jnp.bfloat16)
-    updated = jnp.dot(mix_ref[...], spectral, preferred_element_type=jnp.float32).astype(jnp.bfloat16)
-    out_ref[0] = jnp.dot(updated, full, preferred_element_type=jnp.float32).astype(jnp.bfloat16)
+    full = masked_table(waves, first[pl.program_id(0)], table_ref[0])
+    out_ref[0] = there_and_back(x_ref[0], full, mix_ref[...]).astype(jnp.bfloat16)
 
 
 def transform(values, legendre, mixing, pair_first, waves):
@@ -131,14 +106,138 @@
     )(pair_first, values, legendre, mixing)
 
 
-def mixing_matrix(vertical, fields):
+def swap_groups(parts, lats):
+    lane_group = lax.broadcasted_iota(jnp.int32, parts[0].shape, 1) // lats
+    swapped = []
+    for j in range(len(parts)):
+        merged = None
+        for i, part in enumerate(parts):
+            shift = ((i - j) * lats) % 128
+            turned = pltpu.roll(part, shift, 1) if shift else part
+            merged = turned if merged is None else jnp.where(lane_group == i, turned, merged)
+        swapped.append(merged)
+    return swapped
+
+
+def masked_table(waves, first_wave, table):
+    rows, half = table.shape
+    boundary = waves - first_wave
+    up = lax.broadcasted_iota(jnp.int32, (half, half), 0)
+    across = lax.broadcasted_iota(jnp.int32, (half, half), 1)
+    turn = (up + across == half - 1).astype(jnp.float32).astype(jnp.bfloat16)
+    southern = jnp.dot(table, turn, preferred_element_type=jnp.float32)
+    northern = table.astype(jnp.float32)
+    row_ids = lax.broadcasted_iota(jnp.int32, (rows, half), 0)
+    held = row_ids < boundary
+    degree = jnp.where(held, row_ids, row_ids - boundary)
+    southern = jnp.where(degree % 2 == 0, southern, -southern)
+    zero = jnp.zeros((), jnp.float32)
+    return jnp.concatenate(
+        [
+            jnp.where(held, northern, zero).astype(jnp.bfloat16),
+            jnp.where(held, southern, zero).astype(jnp.bfloat16),
+            jnp.where(held, zero, northern).astype(jnp.bfloat16),
+            jnp.where(held, zero, southern).astype(jnp.bfloat16),
+        ],
+        axis=1,
+    )
+
+
+def there_and_back(values, full, mixing):
+    spectral = lax.dot_general(
+        values, full, (((1,), (1,)), ((), ())), preferred_element_type=jnp.float32
+    ).astype(jnp.bfloat16)
+    updated = jnp.dot(mixing, spectral, preferred_element_type=jnp.float32).astype(jnp.bfloat16)
+    return jnp.dot(updated, full, preferred_element_type=jnp.float32)
+
+
+def packed_kernel(waves, bands, fields, lats, first, x_ref, table_ref, mix_ref, out_ref, held_ref):
+    k = pl.program_id(0)
+    count, tiles = x_ref.shape[1], x_ref.shape[2] // 128
+    group = 128 // lats
+    rows = fields * tiles
+
+    @pl.when(k == 0)
+    def _():
+        @pl.loop(0, bands)
+        def _(band):
+            for field in range(fields):
+                for tile in range(tiles):
+                    at = (field * tiles + tile) * count
+                    held_ref[band, at : at + count, :] = x_ref[
+                        band * fields + field, :, tile * 128 : (tile + 1) * 128
+                    ].astype(jnp.float32)
+
+    def place(slot):
+        return pl.ds(2 * k + slot, rows, stride=count)
+
+    gathered = [[] for _ in range(group)]
+    for slot in range(2):
+        for start in range(0, bands, group):
+            parts = [held_ref[start + i, place(slot), :] for i in range(group)]
+            for j, part in enumerate(swap_groups(parts, lats)):
+                gathered[j].append(part)
+    values = jnp.concatenate([jnp.concatenate(g, axis=1) for g in gathered], axis=0).astype(jnp.bfloat16)
+    full = masked_table(waves, first[k], table_ref[0])
+    result = there_and_back(values, full, mix_ref[...])
+    for slot in range(2):
+        for start in range(0, bands, group):
+            at = (slot * bands + start) * lats
+            parts = [result[j * rows : (j + 1) * rows, at : at + 128] for j in range(group)]
+            for i, part in enumerate(swap_groups(parts, lats)):
+                held_ref[start + i, place(slot), :] = part
+
+    @pl.when(k == pl.num_programs(0) - 1)
+    def _():
+        @pl.loop(0, bands)
+        def _(band):
+            for field in range(fields):
+                for tile in range(tiles):
+                    at = (field * tiles + tile) * count
+                    out_ref[band * fields + field, :, tile * 128 : (tile + 1) * 128] = held_ref[
+                        band, at : at + count, :
+                    ].astype(jnp.bfloat16)
+
+
+def packed_transform(arrived, legendre, mixing, pair_first, waves, bands, fields, lats):
+    total, count, width = arrived.shape
+    pairs, rows, half = legendre.shape
+    columns = mixing.shape[0]
+    flops = 2 * pairs * columns * rows * (4 * bands * lats + columns)
+    whole = pl.BlockSpec((total, count, width), lambda k, first: (0, 0, 0))
+    return pl.pallas_call(
+        functools.partial(packed_kernel, waves, bands, fields, lats),
+        grid_spec=pltpu.PrefetchScalarGridSpec(
+            num_scalar_prefetch=1,
+            grid=(pairs,),
+            in_specs=[
+                whole,
+                pl.BlockSpec((1, rows, half), lambda k, first: (k, 0, 0)),
+                pl.BlockSpec((columns, columns), lambda k, first: (0, 0)),
+            ],
+            out_specs=whole,
+            scratch_shapes=[pltpu.VMEM((bands, fields * width // 128 * count, 128), jnp.float32)],
+        ),
+        out_shape=jax.ShapeDtypeStruct(arrived.shape, jnp.bfloat16),
+        compiler_params=pltpu.CompilerParams(vmem_limit_bytes=52 * 1024 * 1024),
+        cost_estimate=pl.CostEstimate(
+            flops=flops, bytes_accessed=4 * arrived.size + 2 * legendre.size, transcendentals=0
+        ),
+    )(pair_first, arrived, legendre, mixing)
+
+
+def mixing_matrix(vertical, fields, group):
     levels = vertical.shape[1]
     total = 2 * levels
     blocks = jnp.zeros((2, levels, 2, levels), vertical.dtype)
     blocks = blocks.at[0, :, 0, :].set(vertical[0]).at[1, :, 1, :].set(vertical[1])
     block = blocks.reshape(fields, total // fields, fields, total // fields)
     parts = jnp.eye(2, dtype=vertical.dtype)
-    return jnp.einsum("zfyg,cd->zcfydg", block, parts).reshape(2 * total, 2 * total)
+    matrix = jnp.einsum("zfyg,cd->zcfydg", block, parts)
+    if group > 1:
+        tiles = 2 * total // fields // group
+        matrix = matrix.reshape(fields, tiles, group, fields, tiles, group).transpose(2, 0, 1, 5, 3, 4)
+    return matrix.reshape(2 * total, 2 * total)
 
 
 def per_device(fourier, row_length, wave_order, legendre, vertical):
@@ -161,11 +260,18 @@
         choose, flat, (((1,), (1,)), ((), ())), preferred_element_type=jnp.float32
     ).astype(jnp.bfloat16)
     arrived = exchange(outgoing.reshape(total, 2 * pairs, 2 * levels * lats), bands, fields, 0)
-    values = arrived.reshape(bands, fields, pairs, 2, 2 * levels, lats).transpose(2, 1, 4, 3, 0, 5)
-    values = values.reshape(pairs, fields * 2 * levels, 2 * bands * lats)
-    grid_part = transform(values, legendre, mixing_matrix(vertical, fields), pair_first, waves)
-    back = grid_part.reshape(pairs, fields, 2 * levels, 2, bands, lats).transpose(4, 1, 0, 3, 2, 5)
-    home = exchange(back.reshape(total, 2 * pairs, 2 * levels * lats), bands, fields, 1)
+    group = 128 // lats
+    fits = 128 % lats == 0 and bands % group == 0 and 2 * levels % group == 0
+    if fits and (2 * levels // group * fields) % 8 == 0 and 2 * pairs % 16 == 0:
+        mixing = mixing_matrix(vertical, fields, group)
+        back = packed_transform(arrived, legendre, mixing, pair_first, waves, bands, fields, lats)
+    else:
+        values = arrived.reshape(bands, fields, pairs, 2, 2 * levels, lats).transpose(2, 1, 4, 3, 0, 5)
+        values = values.reshape(pairs, fields * 2 * levels, 2 * bands * lats)
+        grid_part = transform(values, legendre, mixing_matrix(vertical, fields, 1), pair_first, waves)
+        back = grid_part.reshape(pairs, fields, 2 * levels, 2, bands, lats).transpose(4, 1, 0, 3, 2, 5)
+        back = back.reshape(total, 2 * pairs, 2 * levels * lats)
+    home = exchange(back, bands, fields, 1)
     restored = lax.dot_general(
         home.reshape(waves, 2 * levels * lats), choose, (((0,), (0,)), ((), ())),
         preferred_element_type=jnp.float32,

time: 433 us -> 332 us (0.77)
  local copies, waits for them, and re-layouts: 147 us -> 22.6 us
  Pallas kernels: 243 us -> 270 us
    reshape x6 -> x2, local copies, waits for them, and re-layouts: 81.4 us -> 7.21 us  [the longest x1 5.89 us: mixing_matrix(): matrix.reshape(fields, tiles, group, fields, tiles, group)]
    transpose x2 -> x1, local copies, waits for them, and re-layouts: 48.7 us -> 8.93 us  [mixing_matrix(): matrix.reshape(fields, tiles, group, fields, tiles, group)]
    pallas_call x1, Pallas kernels: 28.8 us -> 55.2 us  [packed_transform(): pl.pallas_call(functools.partial(packed_kernel, waves, bands, fields, lat...]
    pallas_call x1 -> x0, local copies, waits for them, and re-layouts: 7.98 us -> none  [transform(): pl.pallas_call(functools.partial(pair_kernel, waves), grid_spec=pltpu.Pre...]
where the time goes in v2:
time: 332 us; the launch traced here: 330 us
  Pallas kernels  270 us (81%)
  local copies, waits for them, and re-layouts  22.6 us (7%)
  matrix products  18.8 us (6%)
  other arithmetic  18.6 us (6%)
    pallas_call x2, Pallas kernels, exchange(): pl.pallas_call(functools.partial(exchange_kernel, bands, fields), out_sha...  214 us
    pallas_call x1, Pallas kernels, packed_transform(): pl.pallas_call(functools.partial(packed_kernel, waves, bands, fields, lat...  55.2 us
    select_n x1, other arithmetic, per_device(): return jnp.where(in_range[None, :, None, :], restored, nothing)  10.9 us
    dot_general x1, matrix products, per_device(): lax.dot_general(home.reshape(waves, 2 * levels * lats), choose, (((0,), (...  9.58 us
    dot_general x1, matrix products, per_device(): lax.dot_general(choose, flat, (((1,), (1,)), ((), ())), preferred_element...  9.27 us
    transpose x1, local copies, waits for them, and re-layouts, mixing_matrix(): matrix.reshape(fields, tiles, group, fields, tiles, group)  8.93 us

profile of v2, /device:TPU:11, one launch (start us, length us, event | category | flops | bytes accessed | tf_op | source)
XLA Modules:
  0.0 329.9 jit_solution(11670830236527862479)
XLA Ops:
  0.0 0.8 dynamic_slice.3.first
  0.8 0.7 fusion.3
  1.4 0.1 iota_compare_fusion.3
  1.5 0.0 copy-start.1
  1.5 6.4 %copy_select_fusion = bf16[36,32,2,1024]{3,1,0,2:T(8,128)(2,1)} fusion(bf16[36,32,2,1024]{3,2,1,0:T(2,128)(2,1)} %param.9, pred[32,1024]{1,0:T(8,128)(4,1)S(1)} %iota_compare_fusion.3), kind=kLoop, calls=%fused_computation.4 | loop fusion | flops 2359296 | bytes 9469952 | tf_op jit(solution)/shard_map/jit(_where)/select_n | solution.py:252
  7.9 0.0 copy-done.1
  7.9 0.1 copy.8
  8.1 0.2 eq.18
  8.2 9.3 %convolution_convert_fusion.1 = bf16[1024,2304]{1,0:T(8,128)(2,1)} fusion(bf16[2304,1024]{1,0:T(8,128)(2,1)} %bitcast.20, s32[1024]{0:T(1024)S(1)} %eq.18), kind=kOutput, calls=%fused_computation.2 | convolution fusion | flops 4835246080 | bytes 9441280 | tf_op jit(solution)/shard_map/dot_general | solution.py:259
  17.5 0.0 copy-start
  17.5 107.8 %shard_map.55.x_ref = bf16[32,32,2304]{2,1,0:T(8,128)(2,1)} custom-call(bf16[32,32,2304]{2,1,0:T(8,128)(2,1)} %bitcast.23), custom_call_target="tpu_custom_call" | custom-call | tf_op jit(solution)/shard_map/pallas_call | solution.py:66
  125.3 0.0 copy-done
  125.4 0.1 copy.10
  125.5 0.1 reshape.124
  125.6 0.6 multiply_bitcast_fusion
  126.1 5.9 %reshape.125 = bf16[4,18,4,4,18,4]{5,4,3,2,1,0:T(8,128)(2,1)} reshape(bf16[4,2,36,4,2,36]{5,4,3,2,1,0:T(2,128)(2,1)S(1)} %multiply_bitcast_fusion) | data formatting | bytes 331776 | tf_op jit(solution)/shard_map/reshape | solution.py:239
  132.0 8.9 %copy.11 = bf16[4,4,18,4,4,18]{5,4,3,2,1,0:T(4,128)(2,1)S(1)} copy(bf16[4,4,18,4,4,18]{3,5,4,0,2,1:T(8,128)(2,1)} %bitcast.19) | data formatting | bytes 331776 | tf_op jit(solution)/shard_map/transpose | solution.py:239
  141.0 1.3 reshape.126.mix_ref
  142.3 5.2 %copy.12.table_ref = bf16[16,1025,128]{2,1,0:T(8,128)(2,1)} copy(bf16[16,1025,128]{2,0,1:T(8,128)(2,1)} %param.12) | data formatting | bytes 8396800 | tf_op args[3]
  147.5 55.2 %shard_map.56.src = bf16[32,32,2304]{2,1,0:T(8,128)(2,1)} custom-call(s32[16]{0:T(128)S(1)} %dynamic_slice.3.first, bf16[32,32,2304]{2,1,0:T(8,128)(2,1)} %shard_map.55.x_ref, bf16[16,1025,128]{2,1,0:T(8,128)(2,1)} %copy.12.table_ref, bf16[288,288]{1,0:T(8,128)(2,1)S(1)} %reshape.126.mix_ref), custom_call_target="tpu_custom_call" | custom-call | flops 12393676800 | bytes 13635584 | tf_op jit(solution)/shard_map/pallas_call | solution.py:208
  202.8 106.6 %shard_map.57 = bf16[32,32,2304]{2,1,0:T(8,128)(2,1)} custom-call(bf16[32,32,2304]{2,1,0:T(8,128)(2,1)} %shard_map.56.src), custom_call_target="tpu_custom_call" | custom-call | tf_op jit(solution)/shard_map/pallas_call | solution.py:66
  309.4 9.6 %convolution_convert_fusion = bf16[2304,1024]{1,0:T(8,128)(2,1)} fusion(bf16[1024,2304]{1,0:T(8,128)(2,1)} %bitcast.22, s32[1024]{0:T(1024)S(1)} %eq.18), kind=kOutput, calls=%fused_computation.1 | convolution fusion | flops 4835246080 | bytes 9441280 | tf_op jit(solution)/shard_map/dot_general | solution.py:275
  318.9 10.9 %fusion = bf16[36,32,2,1024]{3,2,1,0:T(2,128)(2,1)} fusion(pred[32,1024]{1,0:T(8,128)(4,1)S(1)} %iota_compare_fusion.3, bf16[2,36,32,1024]{3,2,1,0:T(8,128)(2,1)} %bitcast.21), kind=kLoop, calls=%fused_computation.3 | loop fusion | flops 2359296 | bytes 9469952 | tf_op jit(solution)/shard_map/jit(_where)/select_n | solution.py:280
  (6 shorter events, 0.0 us)
Async XLA Ops:
  1.5 6.4 %copy-start.1 = (s32[512]{0:T(512)S(1)}, s32[512]{0:T(512)}, u32[]{:S(2)}) copy-start(s32[512]{0:T(512)} %param.11) | copy-start | bytes 6148
  17.5 107.9 %copy-start = (bf16[2,72,72]{2,1,0:T(8,128)(2,1)S(1)}, bf16[2,72,72]{2,1,0:T(8,128)(2,1)}, u32[]{:S(2)}) copy-start(bf16[2,72,72]{2,1,0:T(8,128)(2,1)} %param.13) | copy-start | bytes 62212

commit v3 on v2

--- a/solution.py
+++ b/solution.py
@@ -2,6 +2,7 @@
 
 import jax
 import jax.numpy as jnp
+import numpy as np
 from jax import lax
 from jax.experimental import pallas as pl
 from jax.experimental.pallas import tpu as pltpu
@@ -151,62 +152,357 @@
     return jnp.dot(updated, full, preferred_element_type=jnp.float32)
 
 
-def packed_kernel(waves, bands, fields, lats, first, x_ref, table_ref, mix_ref, out_ref, held_ref):
+ROUNDS = (2, 3, 1, 0)
+
+
+def partner(field, turn):
+    if turn == 0:
+        return field
+    if turn == 2:
+        return lax.rem(field + 2, 4)
+    return 3 - field if turn == 3 else field + 1 - 2 * lax.rem(field, 2)
+
+
+def near_equator(band, bands):
+    return (band >= bands // 4) & (band < bands - bands // 4)
+
+
+def greet(band, field, bands):
+    barrier = pltpu.get_barrier_semaphore()
+
+    @pl.loop(1, bands)
+    def _(step):
+        where = (lax.rem(band + step, bands), field)
+        pl.semaphore_signal(barrier, inc=1, device_id=where, device_id_type=MESH)
+
+    for turn in (1, 2, 3):
+        where = (band, partner(field, turn))
+        pl.semaphore_signal(barrier, inc=1, device_id=where, device_id_type=MESH)
+    pl.semaphore_wait(barrier, bands - 1 + 3)
+
+
+def remote(src, dst, send, recv, where):
+    return pltpu.make_async_remote_copy(
+        src_ref=src, dst_ref=dst, send_sem=send, recv_sem=recv, device_id=where, device_id_type=MESH
+    )
+
+
+def outward_kernel(bands, src, dst, mid, plane_send, plane_recv, line_send, line_recv, own_sem):
+    band, field = lax.axis_index("band"), lax.axis_index("field")
+    low, high = bands // 4, bands - bands // 4
+    middle = pl.ds(low, high - low)
+    greet(band, field, bands)
+
+    def landing(turn, slot, origin):
+        return dst.at[field, slot, origin] if turn == 0 else mid.at[turn, slot, origin]
+
+    def plane(turn, step, slot):
+        peer = lax.rem(band + step, bands)
+        return remote(
+            src.at[peer, partner(field, turn), slot], landing(turn, slot, band),
+            plane_send.at[turn, step, slot], plane_recv.at[turn, step, slot], (peer, field),
+        )
+
+    def arrival(turn, step, slot):
+        peer = lax.rem(band + bands - step, bands)
+        spot = landing(turn, slot, peer)
+        return remote(
+            spot, spot, plane_send.at[turn, step, slot], plane_recv.at[turn, step, slot], (peer, field)
+        )
+
+    def own(turn, slot):
+        return pltpu.make_async_copy(
+            src.at[band, partner(field, turn), slot], landing(turn, slot, band), own_sem.at[turn, slot]
+        )
+
+    def line(turn, slot):
+        where = (band, partner(field, turn))
+        if slot == 0:
+            source, target = mid.at[turn, 0], dst.at[field, 0]
+        else:
+            source, target = mid.at[turn, 1, middle], dst.at[field, 1, middle]
+        return remote(source, target, line_send.at[turn, slot], line_recv.at[turn, slot], where)
+
+    def line_arrival(turn, slot):
+        origin = partner(field, turn)
+        spot = dst.at[origin, 0] if slot == 0 else dst.at[origin, 1, middle]
+        return remote(
+            spot, spot, line_send.at[turn, slot], line_recv.at[turn, slot], (band, origin)
+        )
+
+    for turn in ROUNDS:
+        own(turn, 0).start()
+        own(turn, 1).start()
+
+        @pl.loop(1, bands)
+        def _(step):
+            plane(turn, step, 0).start()
+
+            @pl.when(near_equator(band, bands))
+            def _():
+                plane(turn, step, 1).start()
+
+    for turn in ROUNDS:
+        own(turn, 0).wait()
+        own(turn, 1).wait()
+
+        @pl.loop(1, bands)
+        def _(step):
+            arrival(turn, step, 0).wait_recv()
+
+            @pl.when(near_equator(lax.rem(band + bands - step, bands), bands))
+            def _():
+                arrival(turn, step, 1).wait_recv()
+
+        if turn:
+            line(turn, 0).start()
+            line(turn, 1).start()
+
+    for turn in ROUNDS:
+
+        @pl.loop(1, bands)
+        def _(step):
+            plane(turn, step, 0).wait_send()
+
+            @pl.when(near_equator(band, bands))
+            def _():
+                plane(turn, step, 1).wait_send()
+
+        if turn:
+            for slot in range(2):
+                line(turn, slot).wait_send()
+                line_arrival(turn, slot).wait_recv()
+
+
+def homeward_kernel(
+    bands, src, zeros, dst, mid, plane_send, plane_recv, line_send, line_recv, own_sem, zero_sem
+):
+    band, field = lax.axis_index("band"), lax.axis_index("field")
+    low, high = bands // 4, bands - bands // 4
+    middle = pl.ds(low, high - low)
+    greet(band, field, bands)
+
+    def held(turn, slot, target):
+        return src.at[field, slot, target] if turn == 0 else mid.at[turn, slot, target]
+
+    def plane(turn, step, slot):
+        peer = lax.rem(band + step, bands)
+        return remote(
+            held(turn, slot, peer), dst.at[band, partner(field, turn), slot],
+            plane_send.at[turn, step, slot], plane_recv.at[turn, step, slot], (peer, field),
+        )
+
+    def arrival(turn, step, slot):
+        peer = lax.rem(band + bands - step, bands)
+        spot = dst.at[peer, partner(field, turn), slot]
+        return remote(
+            spot, spot, plane_send.at[turn, step, slot], plane_recv.at[turn, step, slot], (peer, field)
+        )
+
+    def own(turn, slot):
+        return pltpu.make_async_copy(
+            held(turn, slot, band), dst.at[band, partner(field, turn), slot], own_sem.at[turn, slot]
+        )
+
+    def blank(peer, z):
+        return pltpu.make_async_copy(zeros, dst.at[peer, z, 1], zero_sem.at[peer, z])
+
+    def line(turn, slot):
+        goal = partner(field, turn)
+        if slot == 0:
+            source, target = src.at[goal, 0], mid.at[turn, 0]
+        else:
+            source, target = src.at[goal, 1, middle], mid.at[turn, 1, middle]
+        return remote(
+            source, target, line_send.at[turn, slot], line_recv.at[turn, slot], (band, goal)
+        )
+
+    for turn in ROUNDS[:3]:
+        line(turn, 0).start()
+        line(turn, 1).start()
+
+    for turn in (0,) + ROUNDS[:3]:
+        if turn:
+            line(turn, 0).wait_recv()
+            line(turn, 1).wait_recv()
+
+        @pl.loop(1, bands)
+        def _(step):
+            plane(turn, step, 0).start()
+
+            @pl.when(near_equator(lax.rem(band + step, bands), bands))
+            def _():
+                plane(turn, step, 1).start()
+
+        own(turn, 0).start()
+
+        @pl.when(near_equator(band, bands))
+        def _():
+            own(turn, 1).start()
+
+    @pl.when(jnp.logical_not(near_equator(band, bands)))
+    def _():
+        @pl.loop(0, bands)
+        def _(peer):
+            for z in range(4):
+                blank(peer, z).start()
+
+        @pl.loop(0, bands)
+        def _(peer):
+            for z in range(4):
+                blank(peer, z).wait()
+
+    for turn in (0,) + ROUNDS[:3]:
+        own(turn, 0).wait()
+
+        @pl.when(near_equator(band, bands))
+        def _():
+            own(turn, 1).wait()
+
+        @pl.loop(1, bands)
+        def _(step):
+            plane(turn, step, 0).wait_send()
+            arrival(turn, step, 0).wait_recv()
+
+            @pl.when(near_equator(lax.rem(band + step, bands), bands))
+            def _():
+                plane(turn, step, 1).wait_send()
+
+            @pl.when(near_equator(band, bands))
+            def _():
+                arrival(turn, step, 1).wait_recv()
+
+        if turn:
+            line(turn, 0).wait_send()
+            line(turn, 1).wait_send()
+
+
+def staged_scratch(bands, piece):
+    return [
+        pltpu.VMEM((4, 2, bands) + piece, jnp.bfloat16),
+        pltpu.SemaphoreType.DMA((4, bands, 2)),
+        pltpu.SemaphoreType.DMA((4, bands, 2)),
+        pltpu.SemaphoreType.DMA((4, 2)),
+        pltpu.SemaphoreType.DMA((4, 2)),
+        pltpu.SemaphoreType.DMA((4, 2)),
+    ]
+
+
+def outward(data):
+    bands, fields, _, count, width = data.shape
+    return pl.pallas_call(
+        functools.partial(outward_kernel, bands),
+        out_shape=jax.ShapeDtypeStruct((fields, 2, bands, count, width), data.dtype),
+        in_specs=[pl.BlockSpec(memory_space=pl.ANY)],
+        out_specs=pl.BlockSpec(memory_space=pl.ANY),
+        scratch_shapes=staged_scratch(bands, (count, width)),
+        compiler_params=pltpu.CompilerParams(
+            collective_id=0, has_side_effects=True, vmem_limit_bytes=12 * 1024 * 1024
+        ),
+    )(data)
+
+
+def homeward(data):
+    fields, _, bands, count, width = data.shape
+    return pl.pallas_call(
+        functools.partial(homeward_kernel, bands),
+        out_shape=jax.ShapeDtypeStruct((bands, fields, 2, count, width), data.dtype),
+        in_specs=[pl.BlockSpec(memory_space=pl.ANY)] * 2,
+        out_specs=pl.BlockSpec(memory_space=pl.ANY),
+        scratch_shapes=staged_scratch(bands, (count, width)) + [pltpu.SemaphoreType.DMA((bands, 4))],
+        compiler_params=pltpu.CompilerParams(
+            collective_id=1, has_side_effects=True, vmem_limit_bytes=12 * 1024 * 1024
+        ),
+    )(data, jnp.zeros((count, width), data.dtype))
+
+
+def compact_table(waves, first_wave, table, spare, shared):
+    rows, half = table.shape
+    boundary = waves - first_wave
+    row_ids = lax.broadcasted_iota(jnp.int32, (rows, half), 0)
+    lanes = lax.broadcasted_iota(jnp.int32, (rows, half), 1)
+    held = row_ids < boundary
+    degree = jnp.where(held, row_ids, row_ids - boundary)
+    even = degree % 2 == 0
+    up = lax.broadcasted_iota(jnp.int32, (half, half), 0)
+    across = lax.broadcasted_iota(jnp.int32, (half, half), 1)
+    turn = (up + across == half - 1).astype(jnp.float32).astype(jnp.bfloat16)
+    origin = jnp.where(across < half // 2, across + half // 2, half + half // 2 - 1 - across)
+    halved = (up == origin).astype(jnp.float32).astype(jnp.bfloat16)
+    northern = table.astype(jnp.float32)
+    zero = jnp.zeros((), jnp.float32)
+    second = jnp.where(held, zero, northern)
+    moved = (lanes == spare) & (first_wave >= waves // 2 - 8)
+    main = jnp.where(moved, second[:, shared : shared + 1], jnp.where(held, northern, zero))
+    main = main.astype(jnp.bfloat16)
+    southern = jnp.dot(main, turn, preferred_element_type=jnp.float32)
+    southern = jnp.where(even, southern, -southern)
+    extra = jnp.dot(second.astype(jnp.bfloat16), halved, preferred_element_type=jnp.float32)
+    extra = jnp.where(even | (lanes < half // 2), extra, -extra)
+    return jnp.concatenate([main, southern.astype(jnp.bfloat16), extra.astype(jnp.bfloat16)], axis=1)
+
+
+def packed_kernel(waves, lats, spare, shared, first, x_ref, table_ref, mix_ref, out_ref, held_ref):
     k = pl.program_id(0)
-    count, tiles = x_ref.shape[1], x_ref.shape[2] // 128
+    fields, _, bands, count, width = x_ref.shape
+    tiles = width // 128
     group = 128 // lats
     rows = fields * tiles
+    low, high = bands // 4, bands - bands // 4
+    spans = [(0, 0, bands, 0), (1, low, high, bands)]
 
     @pl.when(k == 0)
     def _():
-        @pl.loop(0, bands)
-        def _(band):
-            for field in range(fields):
-                for tile in range(tiles):
-                    at = (field * tiles + tile) * count
-                    held_ref[band, at : at + count, :] = x_ref[
-                        band * fields + field, :, tile * 128 : (tile + 1) * 128
-                    ].astype(jnp.float32)
-
-    def place(slot):
-        return pl.ds(2 * k + slot, rows, stride=count)
-
+        for slot, begin, end, base in spans:
+
+            @pl.loop(begin, end)
+            def _(band):
+                for field in range(fields):
+                    for tile in range(tiles):
+                        at = (field * tiles + tile) * count
+                        held_ref[base - begin + band, at : at + count, :] = x_ref[
+                            field, slot, band, :, tile * 128 : (tile + 1) * 128
+                        ].astype(jnp.float32)
+
+    place = pl.ds(k, rows, stride=count)
+    slabs = bands + high - low
     gathered = [[] for _ in range(group)]
-    for slot in range(2):
-        for start in range(0, bands, group):
-            parts = [held_ref[start + i, place(slot), :] for i in range(group)]
-            for j, part in enumerate(swap_groups(parts, lats)):
-                gathered[j].append(part)
+    for start in range(0, slabs, group):
+        parts = [held_ref[start + i, place, :] for i in range(group)]
+        for j, part in enumerate(swap_groups(parts, lats)):
+            gathered[j].append(part)
     values = jnp.concatenate([jnp.concatenate(g, axis=1) for g in gathered], axis=0).astype(jnp.bfloat16)
-    full = masked_table(waves, first[k], table_ref[0])
+    full = compact_table(waves, first[k], table_ref[0], spare, shared)
     result = there_and_back(values, full, mix_ref[...])
-    for slot in range(2):
-        for start in range(0, bands, group):
-            at = (slot * bands + start) * lats
-            parts = [result[j * rows : (j + 1) * rows, at : at + 128] for j in range(group)]
-            for i, part in enumerate(swap_groups(parts, lats)):
-                held_ref[start + i, place(slot), :] = part
+    for start in range(0, slabs, group):
+        at = start * lats
+        parts = [result[j * rows : (j + 1) * rows, at : at + 128] for j in range(group)]
+        for i, part in enumerate(swap_groups(parts, lats)):
+            held_ref[start + i, place, :] = part
 
     @pl.when(k == pl.num_programs(0) - 1)
     def _():
-        @pl.loop(0, bands)
-        def _(band):
-            for field in range(fields):
-                for tile in range(tiles):
-                    at = (field * tiles + tile) * count
-                    out_ref[band * fields + field, :, tile * 128 : (tile + 1) * 128] = held_ref[
-                        band, at : at + count, :
-                    ].astype(jnp.bfloat16)
-
-
-def packed_transform(arrived, legendre, mixing, pair_first, waves, bands, fields, lats):
-    total, count, width = arrived.shape
+        for slot, begin, end, base in spans:
+
+            @pl.loop(begin, end)
+            def _(band):
+                for field in range(fields):
+                    for tile in range(tiles):
+                        at = (field * tiles + tile) * count
+                        out_ref[field, slot, band, :, tile * 128 : (tile + 1) * 128] = held_ref[
+                            base - begin + band, at : at + count, :
+                        ].astype(jnp.bfloat16)
+
+
+def packed_transform(arrived, legendre, mixing, pair_first, waves, lats, spare, shared):
+    fields, _, bands, count, width = arrived.shape
     pairs, rows, half = legendre.shape
     columns = mixing.shape[0]
-    flops = 2 * pairs * columns * rows * (4 * bands * lats + columns)
-    whole = pl.BlockSpec((total, count, width), lambda k, first: (0, 0, 0))
+    flops = 2 * pairs * columns * rows * (3 * bands * lats + columns)
+    whole = pl.BlockSpec(arrived.shape, lambda k, first: (0, 0, 0, 0, 0))
+    slabs = bands + bands - 2 * (bands // 4)
     return pl.pallas_call(
-        functools.partial(packed_kernel, waves, bands, fields, lats),
+        functools.partial(packed_kernel, waves, lats, spare, shared),
         grid_spec=pltpu.PrefetchScalarGridSpec(
             num_scalar_prefetch=1,
             grid=(pairs,),
@@ -216,7 +512,7 @@
                 pl.BlockSpec((columns, columns), lambda k, first: (0, 0)),
             ],
             out_specs=whole,
-            scratch_shapes=[pltpu.VMEM((bands, fields * width // 128 * count, 128), jnp.float32)],
+            scratch_shapes=[pltpu.VMEM((slabs, fields * width // 128 * count, 128), jnp.float32)],
         ),
         out_shape=jax.ShapeDtypeStruct(arrived.shape, jnp.bfloat16),
         compiler_params=pltpu.CompilerParams(vmem_limit_bytes=52 * 1024 * 1024),
@@ -226,58 +522,106 @@
     )(pair_first, arrived, legendre, mixing)
 
 
-def mixing_matrix(vertical, fields, group):
+def mixing_by_rows(vertical, fields, group):
+    levels = vertical.shape[1]
+    per_field = 2 * levels // fields
+    tiles = 2 * per_field // group
+    j, z, t = np.meshgrid(np.arange(group), np.arange(fields), np.arange(tiles), indexing="ij")
+    column = (t * group + j).reshape(-1)
+    part = column // per_field
+    level = z.reshape(-1) * per_field + column % per_field
+    rows = level.size
+    choose = np.zeros((2, rows, levels), np.float32)
+    choose[level // levels, np.arange(rows), level % levels] = 1
+    choose = jnp.asarray(choose, jnp.bfloat16)
+    left = jnp.einsum("qra,qab->rqb", choose, vertical, preferred_element_type=jnp.float32)
+    both = jnp.einsum(
+        "rqb,qsb->rs", left.astype(jnp.bfloat16), choose, preferred_element_type=jnp.float32
+    )
+    return jnp.where(jnp.asarray(part[:, None] == part[None, :]), both, 0.0).astype(jnp.bfloat16)
+
+
+def mixing_matrix(vertical, fields):
     levels = vertical.shape[1]
     total = 2 * levels
     blocks = jnp.zeros((2, levels, 2, levels), vertical.dtype)
     blocks = blocks.at[0, :, 0, :].set(vertical[0]).at[1, :, 1, :].set(vertical[1])
     block = blocks.reshape(fields, total // fields, fields, total // fields)
     parts = jnp.eye(2, dtype=vertical.dtype)
-    matrix = jnp.einsum("zfyg,cd->zcfydg", block, parts)
-    if group > 1:
-        tiles = 2 * total // fields // group
-        matrix = matrix.reshape(fields, tiles, group, fields, tiles, group).transpose(2, 0, 1, 5, 3, 4)
-    return matrix.reshape(2 * total, 2 * total)
+    return jnp.einsum("zfyg,cd->zcfydg", block, parts).reshape(2 * total, 2 * total)
+
+
+def spread_waves(choose, masked):
+    levels, lats, _, waves = masked.shape
+    flat = masked.transpose(2, 0, 1, 3).reshape(2 * levels * lats, waves)
+    return lax.dot_general(
+        choose, flat, (((1,), (1,)), ((), ())), preferred_element_type=jnp.float32
+    ).astype(jnp.bfloat16)
+
+
+def gather_waves(home, choose, shape):
+    levels, lats, _, waves = shape
+    restored = lax.dot_general(
+        home, choose, (((0,), (0,)), ((), ())), preferred_element_type=jnp.float32
+    ).astype(jnp.bfloat16)
+    return restored.reshape(2, levels, lats, waves).transpose(1, 2, 0, 3)
 
 
 def per_device(fourier, row_length, wave_order, legendre, vertical):
     levels, lats, _, waves = fourier.shape
     bands, fields = lax.axis_size("band"), lax.axis_size("field")
+    band = lax.axis_index("band")
     total = bands * fields
-    pairs = legendre.shape[0]
+    pairs, _, half = legendre.shape
     wave_ids = lax.iota(jnp.int32, waves)
     wave_count = jnp.minimum(waves, row_length // 2)
-    in_range = wave_ids[None, :] < wave_count[:, None]
+    in_range = (wave_ids[None, :] < wave_count[:, None])[None, :, None, :]
     nothing = jnp.zeros((), jnp.bfloat16)
-    masked = jnp.where(in_range[None, :, None, :], fourier, nothing)
+    masked = jnp.where(in_range, fourier, nothing)
+    start_pair = (band * fields + lax.axis_index("field")) * pairs
+    pair_first = lax.dynamic_slice_in_dim(wave_order, start_pair, pairs)
+    width = 2 * levels * lats
+
+    if (bands, fields, lats, half, waves, pairs, levels) == (8, 4, 32, 128, 1024, 16, 36):
+        spare, shared, edge = half // 4, half // 2 - 1, waves // 2
+        turned = band >= bands // 2
+        in_band = (band == 1) | (band == bands - 2)
+        spare_lat = jnp.where(turned, lats - 1, 0)
+        shared_lat = jnp.where(turned, 0, lats - 1)
+        lat_ids = lax.iota(jnp.int32, lats)[None, :, None, None]
+        wave_at = wave_ids[None, None, None, :]
+        to_spare = in_band & (lat_ids == spare_lat) & (wave_at >= edge - 8) & (wave_at < edge)
+        to_shared = in_band & (lat_ids == shared_lat) & (wave_at >= edge) & (wave_at < edge + 8)
+        row = lax.dynamic_slice_in_dim(fourier, shared_lat, 1, axis=1)[..., edge : edge + 8]
+        count = lax.dynamic_slice_in_dim(wave_count, shared_lat, 1, axis=0)
+        row = jnp.where(wave_ids[edge : edge + 8] < count[0], row, nothing)
+        pad = ((0, 0), (0, 0), (0, 0), (edge - 8, waves - edge))
+        masked = jnp.where(to_spare, jnp.pad(jnp.flip(row, 3), pad), masked)
+
+        by_holder = wave_order.reshape(total, pairs)
+        ordering = jnp.concatenate([by_holder, waves - 1 - by_holder], axis=1).reshape(waves)
+        choose = (ordering[:, None] == wave_ids[None, :]).astype(jnp.bfloat16)
+        outgoing = spread_waves(choose, masked).reshape(bands, fields, 2, pairs, width)
+        mixing = mixing_by_rows(vertical, fields, 128 // lats)
+        back = packed_transform(
+            outward(outgoing), legendre, mixing, pair_first, waves, lats, spare, shared
+        )
+        restored = gather_waves(homeward(back).reshape(waves, width), choose, fourier.shape)
+        row = lax.dynamic_slice_in_dim(restored, spare_lat, 1, axis=1)[..., edge - 8 : edge]
+        pad = ((0, 0), (0, 0), (0, 0), (edge, waves - edge - 8))
+        restored = jnp.where(to_shared, jnp.pad(jnp.flip(row, 3), pad), restored)
+        return jnp.where(in_range, restored, nothing)
+
     ordering = jnp.stack([wave_order, waves - 1 - wave_order], axis=1).reshape(waves)
     choose = (ordering[:, None] == wave_ids[None, :]).astype(jnp.bfloat16)
-    start_pair = (lax.axis_index("band") * fields + lax.axis_index("field")) * pairs
-    pair_first = lax.dynamic_slice_in_dim(wave_order, start_pair, pairs)
-
-    flat = masked.transpose(2, 0, 1, 3).reshape(2 * levels * lats, waves)
-    outgoing = lax.dot_general(
-        choose, flat, (((1,), (1,)), ((), ())), preferred_element_type=jnp.float32
-    ).astype(jnp.bfloat16)
-    arrived = exchange(outgoing.reshape(total, 2 * pairs, 2 * levels * lats), bands, fields, 0)
-    group = 128 // lats
-    fits = 128 % lats == 0 and bands % group == 0 and 2 * levels % group == 0
-    if fits and (2 * levels // group * fields) % 8 == 0 and 2 * pairs % 16 == 0:
-        mixing = mixing_matrix(vertical, fields, group)
-        back = packed_transform(arrived, legendre, mixing, pair_first, waves, bands, fields, lats)
-    else:
-        values = arrived.reshape(bands, fields, pairs, 2, 2 * levels, lats).transpose(2, 1, 4, 3, 0, 5)
-        values = values.reshape(pairs, fields * 2 * levels, 2 * bands * lats)
-        grid_part = transform(values, legendre, mixing_matrix(vertical, fields, 1), pair_first, waves)
-        back = grid_part.reshape(pairs, fields, 2 * levels, 2, bands, lats).transpose(4, 1, 0, 3, 2, 5)
-        back = back.reshape(total, 2 * pairs, 2 * levels * lats)
-    home = exchange(back, bands, fields, 1)
-    restored = lax.dot_general(
-        home.reshape(waves, 2 * levels * lats), choose, (((0,), (0,)), ((), ())),
-        preferred_element_type=jnp.float32,
-    ).astype(jnp.bfloat16)
-    restored = restored.reshape(2, levels, lats, waves).transpose(1, 2, 0, 3)
-    return jnp.where(in_range[None, :, None, :], restored, nothing)
+    outgoing = spread_waves(choose, masked)
+    arrived = exchange(outgoing.reshape(total, 2 * pairs, width), bands, fields, 2)
+    values = arrived.reshape(bands, fields, pairs, 2, 2 * levels, lats).transpose(2, 1, 4, 3, 0, 5)
+    values = values.reshape(pairs, fields * 2 * levels, 2 * bands * lats)
+    grid_part = transform(values, legendre, mixing_matrix(vertical, fields), pair_first, waves)
+    back = grid_part.reshape(pairs, fields, 2 * levels, 2, bands, lats).transpose(4, 1, 0, 3, 2, 5)
+    home = exchange(back.reshape(total, 2 * pairs, width), bands, fields, 3)
+    return jnp.where(in_range, gather_waves(home.reshape(waves, width), choose, fourier.shape), nothing)
 
 
 def solution(mesh):

time: 332 us -> 301 us (0.907)
  Pallas kernels: 270 us -> 249 us
  matrix products: 18.8 us -> 14 us
  other arithmetic: 18.6 us -> 13.8 us
    pallas_call x3, Pallas kernels: 270 us -> 249 us  [the longest x1 107 us: homeward(): pl.pallas_call(functools.partial(homeward_kernel, bands), out_shape=jax.S...]
    select_n x0 -> x1, local copies, waits for them, and re-layouts: none -> 9.47 us  [per_device(): return jnp.where(in_range, restored, nothing)]
    transpose x1 -> x0, local copies, waits for them, and re-layouts: 8.93 us -> none  [mixing_matrix(): matrix.reshape(fields, tiles, group, fields, tiles, group)]
    reshape x3 -> x1, local copies, waits for them, and re-layouts: 7.31 us -> 0.08 us  [per_device(): by_holder = wave_order.reshape(total, pairs)]
    unnamed x5 -> x16, local copies, waits for them, and re-layouts: 5.24 us -> 12.1 us
    select_n x2 -> x3, other arithmetic: 17.3 us -> 12.1 us  [the longest x1 6.22 us: per_device(): masked = jnp.where(to_spare, jnp.pad(jnp.flip(row, 3), pad), masked)]
    dot_general x2 -> x3, matrix products: 18.8 us -> 14 us  [the longest x1 7.87 us: spread_waves(): lax.dot_general(choose, flat, (((1,), (1,)), ((), ())), preferred_element...]
where the time goes in v3:
time: 301 us; the launch traced here: 300 us
  Pallas kernels  249 us (83%)
  local copies, waits for them, and re-layouts  23.4 us (8%)
  matrix products  14 us (5%)
  other arithmetic  13.8 us (5%)
    pallas_call x1, Pallas kernels, homeward(): pl.pallas_call(functools.partial(homeward_kernel, bands), out_shape=jax.S...  107 us
    pallas_call x1, Pallas kernels, outward(): pl.pallas_call(functools.partial(outward_kernel, bands), out_shape=jax.Sh...  94.9 us
    pallas_call x1, Pallas kernels, packed_transform(): pl.pallas_call(functools.partial(packed_kernel, waves, lats, spare, share...  46.8 us
    unnamed x16, local copies, waits for them, and re-layouts  12.1 us
    select_n x1, local copies, waits for them, and re-layouts, per_device(): return jnp.where(in_range, restored, nothing)  9.47 us
    dot_general x1, matrix products, spread_waves(): lax.dot_general(choose, flat, (((1,), (1,)), ((), ())), preferred_element...  7.87 us
    select_n x1, other arithmetic, per_device(): masked = jnp.where(to_spare, jnp.pad(jnp.flip(row, 3), pad), masked)  6.22 us

profile of v3, /device:TPU:11, one launch (start us, length us, event | category | flops | bytes accessed | tf_op | source)
XLA Modules:
  0.0 300.4 jit_solution(9704148456389920257)
XLA Ops:
  0.0 0.1 and_and_fusion
  0.1 0.7 fusion.6
  0.8 0.6 dynamic_slice.13
  1.4 0.7 slice_compare_fusion
  2.0 0.8 broadcast_select_fusion
  2.8 0.1 rev.7
  2.9 0.1 pad_bitcast_fusion.1
  3.1 0.1 iota_compare_fusion.3
  3.2 6.2 %fusion = bf16[36,32,2,1024]{3,1,0,2:T(8,128)(2,1)} fusion(bf16[36,32,2,1024]{3,2,1,0:T(2,128)(2,1)} %param.7, pred[32,1024]{1,0:T(8,128)(4,1)S(1)} %and_and_fusion, pred[32,1024]{1,0:T(8,128)(4,1)S(1)} %iota_compare_fusion.3, bf16[36,2,1024]{2,0,1:T(8,128)(2,1)S(1)} %copy.11), kind=kLoop, calls=%fused_computation.3 | loop fusion | flops 4718592 | bytes 9650176 | tf_op jit(solution)/shard_map/jit(_where)/select_n | solution.py:599
  9.4 0.1 reshape.172
  9.5 0.1 pad_add_fusion
  9.6 0.1 eq.47
  9.7 7.9 %convolution_convert_fusion.1 = bf16[1024,2304]{1,0:T(8,128)(2,1)S(1)} fusion(bf16[2304,1024]{1,0:T(8,128)(2,1)} %bitcast.34, s32[1024]{0:T(1024)S(1)} %eq.47), kind=kOutput, calls=%fused_computation.1 | convolution fusion | flops 4835246080 | bytes 9441280 | tf_op jit(solution)/shard_map/dot_general | solution.py:557
  17.5 94.9 %shard_map.73.x_ref = bf16[4,2,8,16,2304]{4,3,2,1,0:T(8,128)(2,1)S(1)} custom-call(bf16[8,4,2,16,2304]{4,3,2,1,0:T(8,128)(2,1)S(1)} %bitcast.30), custom_call_target="tpu_custom_call" | custom-call | tf_op jit(solution)/shard_map/pallas_call | solution.py:393
  112.4 0.0 copy-start.1
  112.4 2.2 copy-done.1
  114.6 0.1 dynamic_slice.12.first
  114.7 5.3 %copy.13.table_ref = bf16[16,1025,128]{2,1,0:T(8,128)(2,1)} copy(bf16[16,1025,128]{2,0,1:T(8,128)(2,1)} %param.10) | data formatting | bytes 8396800 | tf_op args[3]
  120.1 0.5 fusion.4.mix_ref
  120.6 46.8 %shard_map.74.src = bf16[4,2,8,16,2304]{4,3,2,1,0:T(8,128)(2,1)} custom-call(s32[16]{0:T(128)S(1)} %dynamic_slice.12.first, bf16[4,2,8,16,2304]{4,3,2,1,0:T(8,128)(2,1)} %copy-done.1, bf16[16,1025,128]{2,1,0:T(8,128)(2,1)} %copy.13.table_ref, bf16[288,288]{1,0:T(8,128)(2,1)S(1)} %fusion.4.mix_ref), custom_call_target="tpu_custom_call" | custom-call | flops 9975398400 | bytes 13635584 | tf_op jit(solution)/shard_map/pallas_call | solution.py:504
  167.4 2.3 copy-done.2
  169.7 107.3 %shard_map.75 = bf16[8,4,2,16,2304]{4,3,2,1,0:T(8,128)(2,1)S(1)} custom-call(bf16[4,2,8,16,2304]{4,3,2,1,0:T(8,128)(2,1)S(1)} %copy-done.2, bf16[16,2304]{1,0:T(8,128)(2,1)S(1)} %broadcast_in_dim.76.zeros), custom_call_target="tpu_custom_call" | custom-call | tf_op jit(solution)/shard_map/pallas_call | solution.py:407
  277.0 5.7 %convolution_convert_fusion = bf16[2304,1024]{1,0:T(8,128)(2,1)S(1)} fusion(bf16[1024,2304]{1,0:T(8,128)(2,1)S(1)} %bitcast.31, s32[1024]{0:T(1024)S(1)} %eq.47), kind=kOutput, calls=%fused_computation | convolution fusion | flops 4835246080 | bytes 9441280 | tf_op jit(solution)/shard_map/dot_general | solution.py:564
  282.7 0.0 copy-start.3
  282.7 2.2 copy-done.3
  284.9 0.3 dynamic-slice_bitcast_fusion
  285.2 0.1 slice.12
  285.3 0.2 rev.8
  285.5 0.1 pad_bitcast_fusion
  285.7 0.1 and_and_fusion.1
  285.7 5.1 %select_select_fusion = bf16[36,32,2,1024]{3,1,0,2:T(8,128)(2,1)} fusion(bf16[36,32,2,1024]{3,1,0,2:T(8,128)(2,1)} %bitcast.33, pred[32,1024]{1,0:T(8,128)(4,1)S(1)} %and_and_fusion.1, pred[32,1024]{1,0:T(8,128)(4,1)S(1)} %iota_compare_fusion.3, bf16[36,2,1024]{2,0,1:T(8,128)(2,1)S(1)} %copy.15), kind=kLoop, calls=%fused_computation.4 | loop fusion | flops 4718592 | bytes 9650176 | tf_op jit(solution)/shard_map/jit(_where)/select_n | solution.py:613
  290.9 9.5 %copy.16 = bf16[36,32,2,1024]{3,2,1,0:T(2,128)(2,1)} copy(bf16[36,32,2,1024]{3,1,0,2:T(8,128)(2,1)} %select_select_fusion) | data formatting | bytes 9437184 | tf_op jit(solution)/shard_map/jit(_where)/select_n | solution.py:613
  (18 shorter events, 0.1 us)
Async XLA Ops:
  0.0 120.0 %copy-start = (bf16[2,72,72]{2,1,0:T(8,128)(2,1)S(1)}, bf16[2,72,72]{2,1,0:T(8,128)(2,1)}, u32[]{:S(2)}) copy-start(bf16[2,72,72]{2,1,0:T(8,128)(2,1)} %param.11) | copy-start | bytes 62212
  3.2 6.2 %copy-start.4 = (s32[512]{0:T(512)S(1)}, s32[512]{0:T(512)}, u32[]{:S(2)}) copy-start(s32[512]{0:T(512)} %param.9) | copy-start | bytes 6148
  112.4 2.2 copy-start.1
  114.6 5.4 %copy-start.5 = (bf16[2,288,72]{1,2,0:T(8,128)(2,1)S(1)}, bf16[2,288,72]{1,2,0:T(8,128)(2,1)}, u32[]{:S(2)}) copy-start(bf16[2,288,72]{1,2,0:T(8,128)(2,1)} %constant.57.clone) | copy-start | bytes 248836
  114.6 5.4 %copy-start.6 = (pred[288,288]{1,0:T(32,128)(4,1)S(1)}, pred[288,288]{1,0:T(32,128)(4,1)}, u32[]{:S(2)}) copy-start(pred[288,288]{1,0:T(32,128)(4,1)} %constant.58.clone) | copy-start | bytes 248836
  167.4 2.3 copy-start.2
  282.7 2.2 copy-start.3

commit v4 on v3

--- a/solution.py
+++ b/solution.py
@@ -187,50 +187,52 @@
     )
 
 
-def outward_kernel(bands, src, dst, mid, plane_send, plane_recv, line_send, line_recv, own_sem):
+def outward_kernel(bands, src, dst, mid, plane_send, plane_recv, line_send, line_recv, own_sem, last_sem):
     band, field = lax.axis_index("band"), lax.axis_index("field")
-    low, high = bands // 4, bands - bands // 4
-    middle = pl.ds(low, high - low)
+    middle = pl.ds(bands // 2 - 1, 2)
     greet(band, field, bands)
-
-    def landing(turn, slot, origin):
-        return dst.at[field, slot, origin] if turn == 0 else mid.at[turn, slot, origin]
 
     def plane(turn, step, slot):
         peer = lax.rem(band + step, bands)
         return remote(
-            src.at[peer, partner(field, turn), slot], landing(turn, slot, band),
+            src.at[peer, partner(field, turn), slot], mid.at[turn, slot, band],
             plane_send.at[turn, step, slot], plane_recv.at[turn, step, slot], (peer, field),
         )
 
     def arrival(turn, step, slot):
         peer = lax.rem(band + bands - step, bands)
-        spot = landing(turn, slot, peer)
+        spot = mid.at[turn, slot, peer]
         return remote(
             spot, spot, plane_send.at[turn, step, slot], plane_recv.at[turn, step, slot], (peer, field)
         )
 
     def own(turn, slot):
         return pltpu.make_async_copy(
-            src.at[band, partner(field, turn), slot], landing(turn, slot, band), own_sem.at[turn, slot]
-        )
+            src.at[band, partner(field, turn), slot], mid.at[turn, slot, band], own_sem.at[turn, slot]
+        )
+
+    def ends(turn, slot, origin):
+        if slot == 0:
+            return mid.at[turn, 0], dst.at[origin, 0]
+        return mid.at[turn, 1, middle], dst.at[origin, 1, middle]
 
     def line(turn, slot):
+        source, target = ends(turn, slot, field)
         where = (band, partner(field, turn))
-        if slot == 0:
-            source, target = mid.at[turn, 0], dst.at[field, 0]
-        else:
-            source, target = mid.at[turn, 1, middle], dst.at[field, 1, middle]
         return remote(source, target, line_send.at[turn, slot], line_recv.at[turn, slot], where)
 
     def line_arrival(turn, slot):
         origin = partner(field, turn)
-        spot = dst.at[origin, 0] if slot == 0 else dst.at[origin, 1, middle]
+        spot = ends(turn, slot, origin)[1]
         return remote(
             spot, spot, line_send.at[turn, slot], line_recv.at[turn, slot], (band, origin)
         )
 
-    for turn in ROUNDS:
+    def last(slot):
+        source, target = ends(0, slot, field)
+        return pltpu.make_async_copy(source, target, last_sem.at[slot])
+
+    def begin(turn):
         own(turn, 0).start()
         own(turn, 1).start()
 
@@ -242,7 +244,8 @@
             def _():
                 plane(turn, step, 1).start()
 
-    for turn in ROUNDS:
+    begin(ROUNDS[0])
+    for at, turn in enumerate(ROUNDS):
         own(turn, 0).wait()
         own(turn, 1).wait()
 
@@ -254,9 +257,15 @@
             def _():
                 arrival(turn, step, 1).wait_recv()
 
-        if turn:
-            line(turn, 0).start()
-            line(turn, 1).start()
+        if at + 1 < len(ROUNDS):
+            begin(ROUNDS[at + 1])
+        for pole, mate in ((0, bands - bands // 4 - 1), (bands - 1, bands // 4)):
+            mid[turn, 0, pole] = mid[turn, 0, pole] + mid[turn, 1, mate]
+        for slot in range(2):
+            if turn:
+                line(turn, slot).start()
+            else:
+                last(slot).start()
 
     for turn in ROUNDS:
 
@@ -268,27 +277,43 @@
             def _():
                 plane(turn, step, 1).wait_send()
 
-        if turn:
-            for slot in range(2):
+        for slot in range(2):
+            if turn:
                 line(turn, slot).wait_send()
                 line_arrival(turn, slot).wait_recv()
+            else:
+                last(slot).wait()
 
 
 def homeward_kernel(
     bands, src, zeros, dst, mid, plane_send, plane_recv, line_send, line_recv, own_sem, zero_sem
 ):
     band, field = lax.axis_index("band"), lax.axis_index("field")
-    low, high = bands // 4, bands - bands // 4
-    middle = pl.ds(low, high - low)
+    middle = pl.ds(bands // 2 - 1, 2)
     greet(band, field, bands)
 
     def held(turn, slot, target):
         return src.at[field, slot, target] if turn == 0 else mid.at[turn, slot, target]
 
-    def plane(turn, step, slot):
+    def second_slot(turn, target, act):
+        north, south = bands // 4, bands - bands // 4 - 1
+
+        @pl.when(target == north)
+        def _():
+            act(held(turn, 0, bands - 1))
+
+        @pl.when(target == south)
+        def _():
+            act(held(turn, 0, 0))
+
+        @pl.when((target > north) & (target < south))
+        def _():
+            act(held(turn, 1, target))
+
+    def plane(turn, step, slot, source):
         peer = lax.rem(band + step, bands)
         return remote(
-            held(turn, slot, peer), dst.at[band, partner(field, turn), slot],
+            source, dst.at[band, partner(field, turn), slot],
             plane_send.at[turn, step, slot], plane_recv.at[turn, step, slot], (peer, field),
         )
 
@@ -299,9 +324,9 @@
             spot, spot, plane_send.at[turn, step, slot], plane_recv.at[turn, step, slot], (peer, field)
         )
 
-    def own(turn, slot):
+    def own(turn, slot, source):
         return pltpu.make_async_copy(
-            held(turn, slot, band), dst.at[band, partner(field, turn), slot], own_sem.at[turn, slot]
+            source, dst.at[band, partner(field, turn), slot], own_sem.at[turn, slot]
         )
 
     def blank(peer, z):
@@ -317,28 +342,20 @@
             source, target, line_send.at[turn, slot], line_recv.at[turn, slot], (band, goal)
         )
 
-    for turn in ROUNDS[:3]:
+    def spread(turn):
+        @pl.loop(1, bands)
+        def _(step):
+            peer = lax.rem(band + step, bands)
+            plane(turn, step, 0, held(turn, 0, peer)).start()
+            second_slot(turn, peer, lambda source: plane(turn, step, 1, source).start())
+
+        own(turn, 0, held(turn, 0, band)).start()
+        second_slot(turn, band, lambda source: own(turn, 1, source).start())
+
+    for turn in (2, 1):
         line(turn, 0).start()
         line(turn, 1).start()
-
-    for turn in (0,) + ROUNDS[:3]:
-        if turn:
-            line(turn, 0).wait_recv()
-            line(turn, 1).wait_recv()
-
-        @pl.loop(1, bands)
-        def _(step):
-            plane(turn, step, 0).start()
-
-            @pl.when(near_equator(lax.rem(band + step, bands), bands))
-            def _():
-                plane(turn, step, 1).start()
-
-        own(turn, 0).start()
-
-        @pl.when(near_equator(band, bands))
-        def _():
-            own(turn, 1).start()
+    spread(0)
 
     @pl.when(jnp.logical_not(near_equator(band, bands)))
     def _():
@@ -347,26 +364,35 @@
             for z in range(4):
                 blank(peer, z).start()
 
+    for slot in range(2):
+        line(2, slot).wait_recv()
+        line(3, slot).start()
+    spread(2)
+    for turn in (1, 3):
+        line(turn, 0).wait_recv()
+        line(turn, 1).wait_recv()
+        spread(turn)
+
+    @pl.when(jnp.logical_not(near_equator(band, bands)))
+    def _():
         @pl.loop(0, bands)
         def _(peer):
             for z in range(4):
                 blank(peer, z).wait()
 
-    for turn in (0,) + ROUNDS[:3]:
-        own(turn, 0).wait()
+    for turn in (0, 2, 1, 3):
+        own(turn, 0, held(turn, 0, band)).wait()
 
         @pl.when(near_equator(band, bands))
         def _():
-            own(turn, 1).wait()
+            own(turn, 1, held(turn, 1, band)).wait()
 
         @pl.loop(1, bands)
         def _(step):
-            plane(turn, step, 0).wait_send()
+            peer = lax.rem(band + step, bands)
+            plane(turn, step, 0, held(turn, 0, peer)).wait_send()
             arrival(turn, step, 0).wait_recv()
-
-            @pl.when(near_equator(lax.rem(band + step, bands), bands))
-            def _():
-                plane(turn, step, 1).wait_send()
+            second_slot(turn, peer, lambda source: plane(turn, step, 1, source).wait_send())
 
             @pl.when(near_equator(band, bands))
             def _():
@@ -395,7 +421,7 @@
         out_shape=jax.ShapeDtypeStruct((fields, 2, bands, count, width), data.dtype),
         in_specs=[pl.BlockSpec(memory_space=pl.ANY)],
         out_specs=pl.BlockSpec(memory_space=pl.ANY),
-        scratch_shapes=staged_scratch(bands, (count, width)),
+        scratch_shapes=staged_scratch(bands, (count, width)) + [pltpu.SemaphoreType.DMA((2,))],
         compiler_params=pltpu.CompilerParams(
             collective_id=0, has_side_effects=True, vmem_limit_bytes=12 * 1024 * 1024
         ),
@@ -432,12 +458,20 @@
     northern = table.astype(jnp.float32)
     zero = jnp.zeros((), jnp.float32)
     second = jnp.where(held, zero, northern)
+    reach = 2 * half // 16 + waves // half * lanes
+    mates = (lanes < half // 4) & (first_wave >= reach)
+    mirror = (up + across == half - half // 4 - 1).astype(jnp.float32).astype(jnp.bfloat16)
+    second_rows = second.astype(jnp.bfloat16)
+    mirrored = jnp.dot(second_rows, mirror, preferred_element_type=jnp.float32)
     moved = (lanes == spare) & (first_wave >= waves // 2 - 8)
     main = jnp.where(moved, second[:, shared : shared + 1], jnp.where(held, northern, zero))
-    main = main.astype(jnp.bfloat16)
-    southern = jnp.dot(main, turn, preferred_element_type=jnp.float32)
-    southern = jnp.where(even, southern, -southern)
-    extra = jnp.dot(second.astype(jnp.bfloat16), halved, preferred_element_type=jnp.float32)
+    main = jnp.where(mates, mirrored, main)
+    southern = jnp.dot(main.astype(jnp.bfloat16), turn, preferred_element_type=jnp.float32)
+    main = jnp.where(mates & jnp.logical_not(even), -main, main).astype(jnp.bfloat16)
+    from_pole = half - 1 - lanes
+    mates = (from_pole < half // 4) & (first_wave >= 2 * half // 16 + waves // half * from_pole)
+    southern = jnp.where(even | mates, southern, -southern)
+    extra = jnp.dot(second_rows, halved, preferred_element_type=jnp.float32)
     extra = jnp.where(even | (lanes < half // 2), extra, -extra)
     return jnp.concatenate([main, southern.astype(jnp.bfloat16), extra.astype(jnp.bfloat16)], axis=1)
 
@@ -449,10 +483,12 @@
     group = 128 // lats
     rows = fields * tiles
     low, high = bands // 4, bands - bands // 4
-    spans = [(0, 0, bands, 0), (1, low, high, bands)]
+    spans = [(0, 0, bands, 0), (1, low + 1, high - 1, bands + 1)]
 
     @pl.when(k == 0)
     def _():
+        held_ref[bands] = jnp.zeros(held_ref.shape[1:], jnp.float32)
+        held_ref[bands + high - low - 1] = jnp.zeros(held_ref.shape[1:], jnp.float32)
         for slot, begin, end, base in spans:
 
             @pl.loop(begin, end)

time: 301 us -> 264 us (0.88)
  Pallas kernels: 249 us -> 213 us
    pallas_call x1, Pallas kernels: 107 us -> 82 us  [homeward(): pl.pallas_call(functools.partial(homeward_kernel, bands), out_shape=jax.S...]
    pallas_call x1, Pallas kernels: 94.9 us -> 82.6 us  [outward(): pl.pallas_call(functools.partial(outward_kernel, bands), out_shape=jax.Sh...]
where the time goes in v4:
time: 264 us
  Pallas kernels  213 us (81%)
  local copies, waits for them, and re-layouts  23.4 us (9%)
  matrix products  14 us (5%)
  other arithmetic  13.8 us (5%)
    pallas_call x1, Pallas kernels, outward(): pl.pallas_call(functools.partial(outward_kernel, bands), out_shape=jax.Sh...  82.6 us
    pallas_call x1, Pallas kernels, homeward(): pl.pallas_call(functools.partial(homeward_kernel, bands), out_shape=jax.S...  82 us
    pallas_call x1, Pallas kernels, packed_transform(): pl.pallas_call(functools.partial(packed_kernel, waves, lats, spare, share...  47.9 us
    unnamed x16, local copies, waits for them, and re-layouts  12.1 us
    select_n x1, local copies, waits for them, and re-layouts, per_device(): return jnp.where(in_range, restored, nothing)  9.47 us
    dot_general x1, matrix products, spread_waves(): lax.dot_general(choose, flat, (((1,), (1,)), ((), ())), preferred_element...  7.87 us
    select_n x1, other arithmetic, per_device(): masked = jnp.where(to_spare, jnp.pad(jnp.flip(row, 3), pad), masked)  6.22 us
    dot_general x1, matrix products, gather_waves(): lax.dot_general(home, choose, (((0,), (0,)), ((), ())), preferred_element...  5.65 us

profile of v4, /device:TPU:11, one launch (start us, length us, event | category | flops | bytes accessed | tf_op | source)
XLA Modules:
  0.0 263.9 jit_solution(13070553463862616286)
XLA Ops:
  0.0 0.1 and_and_fusion
  0.1 0.7 fusion.6
  0.8 0.6 dynamic_slice.13
  1.4 0.7 slice_compare_fusion
  2.0 0.8 broadcast_select_fusion
  2.8 0.1 rev.7
  2.9 0.1 pad_bitcast_fusion.1
  3.1 0.1 iota_compare_fusion.3
  3.2 0.0 copy-start.4
  3.2 6.2 %fusion = bf16[36,32,2,1024]{3,1,0,2:T(8,128)(2,1)} fusion(bf16[36,32,2,1024]{3,2,1,0:T(2,128)(2,1)} %param.7, pred[32,1024]{1,0:T(8,128)(4,1)S(1)} %and_and_fusion, pred[32,1024]{1,0:T(8,128)(4,1)S(1)} %iota_compare_fusion.3, bf16[36,2,1024]{2,0,1:T(8,128)(2,1)S(1)} %copy.11), kind=kLoop, calls=%fused_computation.3 | loop fusion | flops 4718592 | bytes 9650176 | tf_op jit(solution)/shard_map/jit(_where)/select_n | solution.py:635
  9.4 0.1 reshape.172
  9.5 0.1 pad_add_fusion
  9.6 0.1 eq.47
  9.7 7.9 %convolution_convert_fusion.1 = bf16[1024,2304]{1,0:T(8,128)(2,1)S(1)} fusion(bf16[2304,1024]{1,0:T(8,128)(2,1)} %bitcast.34, s32[1024]{0:T(1024)S(1)} %eq.47), kind=kOutput, calls=%fused_computation.1 | convolution fusion | flops 4835246080 | bytes 9441280 | tf_op jit(solution)/shard_map/dot_general | solution.py:593
  17.5 82.6 %shard_map.73.x_ref = bf16[4,2,8,16,2304]{4,3,2,1,0:T(8,128)(2,1)S(1)} custom-call(bf16[8,4,2,16,2304]{4,3,2,1,0:T(8,128)(2,1)S(1)} %bitcast.30), custom_call_target="tpu_custom_call" | custom-call | tf_op jit(solution)/shard_map/pallas_call | solution.py:419
  100.1 0.0 copy-start.1
  100.2 2.2 copy-done.1
  102.3 0.1 dynamic_slice.12.first
  102.4 5.3 %copy.13.table_ref = bf16[16,1025,128]{2,1,0:T(8,128)(2,1)} copy(bf16[16,1025,128]{2,0,1:T(8,128)(2,1)} %param.10) | data formatting | bytes 8396800 | tf_op args[3]
  107.8 0.5 fusion.4.mix_ref
  108.3 47.9 %shard_map.74.src = bf16[4,2,8,16,2304]{4,3,2,1,0:T(8,128)(2,1)} custom-call(s32[16]{0:T(128)S(1)} %dynamic_slice.12.first, bf16[4,2,8,16,2304]{4,3,2,1,0:T(8,128)(2,1)} %copy-done.1, bf16[16,1025,128]{2,1,0:T(8,128)(2,1)} %copy.13.table_ref, bf16[288,288]{1,0:T(8,128)(2,1)S(1)} %fusion.4.mix_ref), custom_call_target="tpu_custom_call" | custom-call | flops 9975398400 | bytes 13635584 | tf_op jit(solution)/shard_map/pallas_call | solution.py:540
  156.2 2.3 copy-done.2
  158.6 82.0 %shard_map.75 = bf16[8,4,2,16,2304]{4,3,2,1,0:T(8,128)(2,1)S(1)} custom-call(bf16[4,2,8,16,2304]{4,3,2,1,0:T(8,128)(2,1)S(1)} %copy-done.2, bf16[16,2304]{1,0:T(8,128)(2,1)S(1)} %broadcast_in_dim.76.zeros), custom_call_target="tpu_custom_call" | custom-call | tf_op jit(solution)/shard_map/pallas_call | solution.py:433
  240.6 5.6 %convolution_convert_fusion = bf16[2304,1024]{1,0:T(8,128)(2,1)S(1)} fusion(bf16[1024,2304]{1,0:T(8,128)(2,1)S(1)} %bitcast.31, s32[1024]{0:T(1024)S(1)} %eq.47), kind=kOutput, calls=%fused_computation | convolution fusion | flops 4835246080 | bytes 9441280 | tf_op jit(solution)/shard_map/dot_general | solution.py:600
  246.2 2.2 copy-done.3
  248.4 0.3 dynamic-slice_bitcast_fusion
  248.7 0.1 slice.12
  248.9 0.2 rev.8
  249.1 0.1 pad_bitcast_fusion
  249.2 0.1 and_and_fusion.1
  249.3 5.1 %select_select_fusion = bf16[36,32,2,1024]{3,1,0,2:T(8,128)(2,1)} fusion(bf16[36,32,2,1024]{3,1,0,2:T(8,128)(2,1)} %bitcast.33, pred[32,1024]{1,0:T(8,128)(4,1)S(1)} %and_and_fusion.1, pred[32,1024]{1,0:T(8,128)(4,1)S(1)} %iota_compare_fusion.3, bf16[36,2,1024]{2,0,1:T(8,128)(2,1)S(1)} %copy.15), kind=kLoop, calls=%fused_computation.4 | loop fusion | flops 4718592 | bytes 9650176 | tf_op jit(solution)/shard_map/jit(_where)/select_n | solution.py:649
  254.4 9.5 %copy.16 = bf16[36,32,2,1024]{3,2,1,0:T(2,128)(2,1)} copy(bf16[36,32,2,1024]{3,1,0,2:T(8,128)(2,1)} %select_select_fusion) | data formatting | bytes 9437184 | tf_op jit(solution)/shard_map/jit(_where)/select_n | solution.py:649
  (18 shorter events, 0.1 us)
Async XLA Ops:
  0.0 107.8 %copy-start = (bf16[2,72,72]{2,1,0:T(8,128)(2,1)S(1)}, bf16[2,72,72]{2,1,0:T(8,128)(2,1)}, u32[]{:S(2)}) copy-start(bf16[2,72,72]{2,1,0:T(8,128)(2,1)} %param.11) | copy-start | bytes 62212
  3.2 6.2 %copy-start.4 = (s32[512]{0:T(512)S(1)}, s32[512]{0:T(512)}, u32[]{:S(2)}) copy-start(s32[512]{0:T(512)} %param.9) | copy-start | bytes 6148
  100.1 2.2 copy-start.1
  102.3 5.4 %copy-start.5 = (bf16[2,288,72]{1,2,0:T(8,128)(2,1)S(1)}, bf16[2,288,72]{1,2,0:T(8,128)(2,1)}, u32[]{:S(2)}) copy-start(bf16[2,288,72]{1,2,0:T(8,128)(2,1)} %constant.57.clone) | copy-start | bytes 248836
  102.3 5.4 %copy-start.6 = (pred[288,288]{1,0:T(32,128)(4,1)S(1)}, pred[288,288]{1,0:T(32,128)(4,1)}, u32[]{:S(2)}) copy-start(pred[288,288]{1,0:T(32,128)(4,1)} %constant.58.clone) | copy-start | bytes 248836
  156.2 2.3 copy-start.2
  246.2 2.2 copy-start.3

commit v5 on v4

--- a/solution.py
+++ b/solution.py
@@ -442,41 +442,48 @@
     )(data, jnp.zeros((count, width), data.dtype))
 
 
-def compact_table(waves, first_wave, table, spare, shared):
+def lane_origins(half):
+    lane = np.arange(half)
+    columns = [
+        half - 1 - lane,
+        np.where(lane < half // 2, lane + half // 2, half + half // 2 - 1 - lane),
+        half - half // 4 - 1 - lane,
+        lane - half // 4,
+    ]
+    return (np.arange(half)[:, None] == np.concatenate(columns)[None, :]).astype(np.float32)
+
+
+def compact_table(waves, first_wave, table, select, spare):
     rows, half = table.shape
     boundary = waves - first_wave
     row_ids = lax.broadcasted_iota(jnp.int32, (rows, half), 0)
-    lanes = lax.broadcasted_iota(jnp.int32, (rows, half), 1)
+    lanes = lax.broadcasted_iota(jnp.int32, (1, half), 1)
     held = row_ids < boundary
     degree = jnp.where(held, row_ids, row_ids - boundary)
-    even = degree % 2 == 0
-    up = lax.broadcasted_iota(jnp.int32, (half, half), 0)
-    across = lax.broadcasted_iota(jnp.int32, (half, half), 1)
-    turn = (up + across == half - 1).astype(jnp.float32).astype(jnp.bfloat16)
-    origin = jnp.where(across < half // 2, across + half // 2, half + half // 2 - 1 - across)
-    halved = (up == origin).astype(jnp.float32).astype(jnp.bfloat16)
-    northern = table.astype(jnp.float32)
-    zero = jnp.zeros((), jnp.float32)
-    second = jnp.where(held, zero, northern)
-    reach = 2 * half // 16 + waves // half * lanes
-    mates = (lanes < half // 4) & (first_wave >= reach)
-    mirror = (up + across == half - half // 4 - 1).astype(jnp.float32).astype(jnp.bfloat16)
-    second_rows = second.astype(jnp.bfloat16)
-    mirrored = jnp.dot(second_rows, mirror, preferred_element_type=jnp.float32)
-    moved = (lanes == spare) & (first_wave >= waves // 2 - 8)
-    main = jnp.where(moved, second[:, shared : shared + 1], jnp.where(held, northern, zero))
-    main = jnp.where(mates, mirrored, main)
-    southern = jnp.dot(main.astype(jnp.bfloat16), turn, preferred_element_type=jnp.float32)
-    main = jnp.where(mates & jnp.logical_not(even), -main, main).astype(jnp.bfloat16)
-    from_pole = half - 1 - lanes
-    mates = (from_pole < half // 4) & (first_wave >= 2 * half // 16 + waves // half * from_pole)
-    southern = jnp.where(even | mates, southern, -southern)
-    extra = jnp.dot(second_rows, halved, preferred_element_type=jnp.float32)
-    extra = jnp.where(even | (lanes < half // 2), extra, -extra)
-    return jnp.concatenate([main, southern.astype(jnp.bfloat16), extra.astype(jnp.bfloat16)], axis=1)
-
-
-def packed_kernel(waves, lats, spare, shared, first, x_ref, table_ref, mix_ref, out_ref, held_ref):
+    sign = (1 - 2 * (degree % 2)).astype(jnp.float32)
+    variants = jnp.dot(table.astype(jnp.bfloat16), select, preferred_element_type=jnp.float32)
+    turned, extra, mirrored, mirrored_south = [
+        variants[:, i * half : (i + 1) * half] for i in range(4)
+    ]
+
+    def shares(from_pole):
+        mates = (from_pole < half // 4) & (first_wave >= half // 8 + waves // half * from_pole)
+        moved = (from_pole == spare) & (first_wave >= waves // 2 - 8)
+        mates, moved = mates.astype(jnp.float32), moved.astype(jnp.float32)
+        return mates, moved, 1.0 - mates - moved
+
+    mates, moved, kept = shares(lanes)
+    main = jnp.where(held, table * kept, mirrored * (sign * mates + moved))
+    mates, moved, kept = shares(half - 1 - lanes)
+    southern = jnp.where(held, turned * (sign * kept), mirrored_south * (mates + sign * moved))
+    upper = (lanes < half // 2).astype(jnp.float32)
+    extra = jnp.where(held, 0.0, extra * (upper + sign * (1.0 - upper)))
+    return jnp.concatenate([main, southern, extra], axis=1).astype(jnp.bfloat16)
+
+
+def packed_kernel(
+    waves, lats, spare, first, x_ref, table_ref, mix_ref, select_ref, out_ref, held_ref, wide_ref
+):
     k = pl.program_id(0)
     fields, _, bands, count, width = x_ref.shape
     tiles = width // 128
@@ -487,6 +494,15 @@
 
     @pl.when(k == 0)
     def _():
+        row_total, pairs, half = table_ref.shape
+        step = next(n for n in range(32, 0, -1) if row_total % n == 0)
+
+        @pl.loop(0, row_total // step)
+        def _(i):
+            block = table_ref[pl.ds(i * step, step)].astype(jnp.float32)
+            at = pl.multiple_of(i * (step * pairs), step * pairs)
+            wide_ref[pl.ds(at, step * pairs), :] = block.reshape(step * pairs, half)
+
         held_ref[bands] = jnp.zeros(held_ref.shape[1:], jnp.float32)
         held_ref[bands + high - low - 1] = jnp.zeros(held_ref.shape[1:], jnp.float32)
         for slot, begin, end, base in spans:
@@ -508,8 +524,13 @@
         for j, part in enumerate(swap_groups(parts, lats)):
             gathered[j].append(part)
     values = jnp.concatenate([jnp.concatenate(g, axis=1) for g in gathered], axis=0).astype(jnp.bfloat16)
-    full = compact_table(waves, first[k], table_ref[0], spare, shared)
-    result = there_and_back(values, full, mix_ref[...])
+    table = wide_ref[pl.ds(k, table_ref.shape[0], stride=table_ref.shape[1]), :]
+    full = compact_table(waves, first[k], table, select_ref[...], spare)
+    mixed = jnp.dot(mix_ref[...], values, preferred_element_type=jnp.float32).astype(jnp.bfloat16)
+    updated = lax.dot_general(
+        mixed, full, (((1,), (1,)), ((), ())), preferred_element_type=jnp.float32
+    ).astype(jnp.bfloat16)
+    result = jnp.dot(updated, full, preferred_element_type=jnp.float32)
     for start in range(0, slabs, group):
         at = start * lats
         parts = [result[j * rows : (j + 1) * rows, at : at + 128] for j in range(group)]
@@ -530,32 +551,37 @@
                         ].astype(jnp.bfloat16)
 
 
-def packed_transform(arrived, legendre, mixing, pair_first, waves, lats, spare, shared):
+def packed_transform(arrived, legendre, mixing, pair_first, waves, lats, spare):
     fields, _, bands, count, width = arrived.shape
     pairs, rows, half = legendre.shape
     columns = mixing.shape[0]
     flops = 2 * pairs * columns * rows * (3 * bands * lats + columns)
     whole = pl.BlockSpec(arrived.shape, lambda k, first: (0, 0, 0, 0, 0))
     slabs = bands + bands - 2 * (bands // 4)
+    select = jnp.asarray(lane_origins(half), jnp.bfloat16)
     return pl.pallas_call(
-        functools.partial(packed_kernel, waves, lats, spare, shared),
+        functools.partial(packed_kernel, waves, lats, spare),
         grid_spec=pltpu.PrefetchScalarGridSpec(
             num_scalar_prefetch=1,
             grid=(pairs,),
             in_specs=[
                 whole,
-                pl.BlockSpec((1, rows, half), lambda k, first: (k, 0, 0)),
+                pl.BlockSpec((rows, pairs, half), lambda k, first: (0, 0, 0)),
                 pl.BlockSpec((columns, columns), lambda k, first: (0, 0)),
+                pl.BlockSpec(select.shape, lambda k, first: (0, 0)),
             ],
             out_specs=whole,
-            scratch_shapes=[pltpu.VMEM((slabs, fields * width // 128 * count, 128), jnp.float32)],
+            scratch_shapes=[
+                pltpu.VMEM((slabs, fields * width // 128 * count, 128), jnp.float32),
+                pltpu.VMEM((rows * pairs, half), jnp.float32),
+            ],
         ),
         out_shape=jax.ShapeDtypeStruct(arrived.shape, jnp.bfloat16),
-        compiler_params=pltpu.CompilerParams(vmem_limit_bytes=52 * 1024 * 1024),
+        compiler_params=pltpu.CompilerParams(vmem_limit_bytes=56 * 1024 * 1024),
         cost_estimate=pl.CostEstimate(
             flops=flops, bytes_accessed=4 * arrived.size + 2 * legendre.size, transcendentals=0
         ),
-    )(pair_first, arrived, legendre, mixing)
+    )(pair_first, arrived, legendre.transpose(1, 0, 2), mixing, select)
 
 
 def mixing_by_rows(vertical, fields, group):
@@ -619,7 +645,7 @@
     width = 2 * levels * lats
 
     if (bands, fields, lats, half, waves, pairs, levels) == (8, 4, 32, 128, 1024, 16, 36):
-        spare, shared, edge = half // 4, half // 2 - 1, waves // 2
+        spare, edge = half // 4, waves // 2
         turned = band >= bands // 2
         in_band = (band == 1) | (band == bands - 2)
         spare_lat = jnp.where(turned, lats - 1, 0)
@@ -640,7 +666,7 @@
         outgoing = spread_waves(choose, masked).reshape(bands, fields, 2, pairs, width)
         mixing = mixing_by_rows(vertical, fields, 128 // lats)
         back = packed_transform(
-            outward(outgoing), legendre, mixing, pair_first, waves, lats, spare, shared
+            outward(outgoing), legendre, mixing, pair_first, waves, lats, spare
         )
         restored = gather_waves(homeward(back).reshape(waves, width), choose, fourier.shape)
         row = lax.dynamic_slice_in_dim(restored, spare_lat, 1, axis=1)[..., edge - 8 : edge]

time: 264 us -> 260 us (0.985)
  local copies, waits for them, and re-layouts: 23.4 us -> 18.6 us
    unnamed x16 -> x15, local copies, waits for them, and re-layouts: 12.1 us -> 6.74 us
where the time goes in v5:
time: 260 us
  Pallas kernels  213 us (82%)
  local copies, waits for them, and re-layouts  18.6 us (7%)
  matrix products  14.7 us (6%)
  other arithmetic  13.8 us (5%)
    pallas_call x1, Pallas kernels, outward(): pl.pallas_call(functools.partial(outward_kernel, bands), out_shape=jax.Sh...  82.6 us
    pallas_call x1, Pallas kernels, homeward(): pl.pallas_call(functools.partial(homeward_kernel, bands), out_shape=jax.S...  82 us
    pallas_call x1, Pallas kernels, packed_transform(): pl.pallas_call(functools.partial(packed_kernel, waves, lats, spare), grid...  48 us
    select_n x1, local copies, waits for them, and re-layouts, per_device(): return jnp.where(in_range, restored, nothing)  9.47 us
    dot_general x1, matrix products, spread_waves(): lax.dot_general(choose, flat, (((1,), (1,)), ((), ())), preferred_element...  7.86 us
    unnamed x15, local copies, waits for them, and re-layouts  6.74 us
    select_n x1, other arithmetic, per_device(): masked = jnp.where(to_spare, jnp.pad(jnp.flip(row, 3), pad), masked)  6.22 us
    dot_general x1, matrix products, gather_waves(): lax.dot_general(home, choose, (((0,), (0,)), ((), ())), preferred_element...  5.65 us

profile of v5, /device:TPU:11, one launch (start us, length us, event | category | flops | bytes accessed | tf_op | source)
XLA Modules:
  0.0 259.9 jit_solution(13172946897222649668)
XLA Ops:
  0.0 0.1 and_and_fusion
  0.1 0.7 fusion.6
  0.8 0.6 dynamic_slice.13
  1.4 0.7 slice_compare_fusion
  2.0 0.8 broadcast_select_fusion
  2.8 0.1 rev.7
  2.9 0.1 pad_bitcast_fusion.1
  3.1 0.1 iota_compare_fusion.3
  3.2 6.2 %fusion = bf16[36,32,2,1024]{3,1,0,2:T(8,128)(2,1)} fusion(bf16[36,32,2,1024]{3,2,1,0:T(2,128)(2,1)} %param.8, pred[32,1024]{1,0:T(8,128)(4,1)S(1)} %and_and_fusion, pred[32,1024]{1,0:T(8,128)(4,1)S(1)} %iota_compare_fusion.3, bf16[36,2,1024]{2,0,1:T(8,128)(2,1)S(1)} %copy.11), kind=kLoop, calls=%fused_computation.3 | loop fusion | flops 4718592 | bytes 9650176 | tf_op jit(solution)/shard_map/jit(_where)/select_n | solution.py:661
  9.4 0.1 reshape.172
  9.5 0.1 pad_add_fusion
  9.6 0.1 eq.47
  9.7 7.9 %convolution_convert_fusion.1 = bf16[1024,2304]{1,0:T(8,128)(2,1)S(1)} fusion(bf16[2304,1024]{1,0:T(8,128)(2,1)} %bitcast.35, s32[1024]{0:T(1024)S(1)} %eq.47), kind=kOutput, calls=%fused_computation.1 | convolution fusion | flops 4835246080 | bytes 9441280 | tf_op jit(solution)/shard_map/dot_general | solution.py:619
  17.5 0.0 copy-start.5
  17.5 0.0 copy-start.6
  17.5 82.6 %shard_map.82.x_ref = bf16[4,2,8,16,2304]{4,3,2,1,0:T(8,128)(2,1)S(1)} custom-call(bf16[8,4,2,16,2304]{4,3,2,1,0:T(8,128)(2,1)S(1)} %bitcast.31), custom_call_target="tpu_custom_call" | custom-call | tf_op jit(solution)/shard_map/pallas_call | solution.py:419
  100.2 2.2 copy-done.1
  102.4 0.6 dynamic_slice.12.first
  103.0 1.2 fusion.4.mix_ref
  104.2 48.0 %shard_map.83.src = bf16[4,2,8,16,2304]{4,3,2,1,0:T(8,128)(2,1)} custom-call(s32[16]{0:T(128)} %dynamic_slice.12.first, bf16[4,2,8,16,2304]{4,3,2,1,0:T(8,128)(2,1)} %copy-done.1, bf16[1025,16,128]{2,1,0:T(8,128)(2,1)} %bitcast.36, bf16[288,288]{1,0:T(8,128)(2,1)} %fusion.4.mix_ref, bf16[128,512]{1,0:T(8,128)(2,1)} %constant.61.clone.select_ref), custom_call_target="tpu_custom_call" | custom-call | flops 9975398400 | bytes 13635584 | tf_op jit(solution)/shard_map/pallas_call | solution.py:562
  152.2 2.3 copy-done.2
  154.6 82.0 %shard_map.84 = bf16[8,4,2,16,2304]{4,3,2,1,0:T(8,128)(2,1)S(1)} custom-call(bf16[4,2,8,16,2304]{4,3,2,1,0:T(8,128)(2,1)S(1)} %copy-done.2, bf16[16,2304]{1,0:T(8,128)(2,1)S(1)} %broadcast_in_dim.76.zeros), custom_call_target="tpu_custom_call" | custom-call | tf_op jit(solution)/shard_map/pallas_call | solution.py:433
  236.6 5.6 %convolution_convert_fusion = bf16[2304,1024]{1,0:T(8,128)(2,1)S(1)} fusion(bf16[1024,2304]{1,0:T(8,128)(2,1)S(1)} %bitcast.32, s32[1024]{0:T(1024)S(1)} %eq.47), kind=kOutput, calls=%fused_computation | convolution fusion | flops 4835246080 | bytes 9441280 | tf_op jit(solution)/shard_map/dot_general | solution.py:626
  242.2 0.0 copy-start.3
  242.3 2.2 copy-done.3
  244.4 0.3 dynamic-slice_bitcast_fusion
  244.7 0.1 slice.12
  244.9 0.2 rev.8
  245.1 0.1 pad_bitcast_fusion
  245.2 0.1 and_and_fusion.1
  245.3 5.1 %select_select_fusion = bf16[36,32,2,1024]{3,1,0,2:T(8,128)(2,1)} fusion(bf16[36,32,2,1024]{3,1,0,2:T(8,128)(2,1)} %bitcast.34, pred[32,1024]{1,0:T(8,128)(4,1)S(1)} %and_and_fusion.1, pred[32,1024]{1,0:T(8,128)(4,1)S(1)} %iota_compare_fusion.3, bf16[36,2,1024]{2,0,1:T(8,128)(2,1)S(1)} %copy.14), kind=kLoop, calls=%fused_computation.4 | loop fusion | flops 4718592 | bytes 9650176 | tf_op jit(solution)/shard_map/jit(_where)/select_n | solution.py:675
  250.5 9.5 %copy.15 = bf16[36,32,2,1024]{3,2,1,0:T(2,128)(2,1)} copy(bf16[36,32,2,1024]{3,1,0,2:T(8,128)(2,1)} %select_select_fusion) | data formatting | bytes 9437184 | tf_op jit(solution)/shard_map/jit(_where)/select_n | solution.py:675
  (17 shorter events, 0.1 us)
Async XLA Ops:
  0.0 103.0 %copy-start = (bf16[2,72,72]{2,1,0:T(8,128)(2,1)S(1)}, bf16[2,72,72]{2,1,0:T(8,128)(2,1)}, u32[]{:S(2)}) copy-start(bf16[2,72,72]{2,1,0:T(8,128)(2,1)} %param.12) | copy-start | bytes 62212
  3.2 6.2 %copy-start.4 = (s32[512]{0:T(512)S(1)}, s32[512]{0:T(512)}, u32[]{:S(2)}) copy-start(s32[512]{0:T(512)} %param.10) | copy-start | bytes 6148
  17.5 85.4 %copy-start.5 = (bf16[2,288,72]{1,2,0:T(8,128)(2,1)S(1)}, bf16[2,288,72]{1,2,0:T(8,128)(2,1)}, u32[]{:S(2)}) copy-start(bf16[2,288,72]{1,2,0:T(8,128)(2,1)} %constant.59.clone) | copy-start | bytes 248836
  17.5 85.4 %copy-start.6 = (pred[288,288]{1,0:T(32,128)(4,1)S(1)}, pred[288,288]{1,0:T(32,128)(4,1)}, u32[]{:S(2)}) copy-start(pred[288,288]{1,0:T(32,128)(4,1)} %constant.60.clone) | copy-start | bytes 248836
  100.2 2.2 copy-start.1
  152.2 2.3 copy-start.2
  242.2 2.2 copy-start.3

commit v6 on v5

--- a/solution.py
+++ b/solution.py
@@ -500,8 +500,8 @@
         @pl.loop(0, row_total // step)
         def _(i):
             block = table_ref[pl.ds(i * step, step)].astype(jnp.float32)
-            at = pl.multiple_of(i * (step * pairs), step * pairs)
-            wide_ref[pl.ds(at, step * pairs), :] = block.reshape(step * pairs, half)
+            for n in range(step):
+                wide_ref[pl.ds((i * step + n) * (pairs + 1), pairs), :] = block[n]
 
         held_ref[bands] = jnp.zeros(held_ref.shape[1:], jnp.float32)
         held_ref[bands + high - low - 1] = jnp.zeros(held_ref.shape[1:], jnp.float32)
@@ -511,12 +511,12 @@
             def _(band):
                 for field in range(fields):
                     for tile in range(tiles):
-                        at = (field * tiles + tile) * count
+                        at = (field * tiles + tile) * (count + 1)
                         held_ref[base - begin + band, at : at + count, :] = x_ref[
                             field, slot, band, :, tile * 128 : (tile + 1) * 128
                         ].astype(jnp.float32)
 
-    place = pl.ds(k, rows, stride=count)
+    place = pl.ds(k, rows, stride=count + 1)
     slabs = bands + high - low
     gathered = [[] for _ in range(group)]
     for start in range(0, slabs, group):
@@ -524,13 +524,9 @@
         for j, part in enumerate(swap_groups(parts, lats)):
             gathered[j].append(part)
     values = jnp.concatenate([jnp.concatenate(g, axis=1) for g in gathered], axis=0).astype(jnp.bfloat16)
-    table = wide_ref[pl.ds(k, table_ref.shape[0], stride=table_ref.shape[1]), :]
+    table = wide_ref[pl.ds(k, table_ref.shape[0], stride=table_ref.shape[1] + 1), :]
     full = compact_table(waves, first[k], table, select_ref[...], spare)
-    mixed = jnp.dot(mix_ref[...], values, preferred_element_type=jnp.float32).astype(jnp.bfloat16)
-    updated = lax.dot_general(
-        mixed, full, (((1,), (1,)), ((), ())), preferred_element_type=jnp.float32
-    ).astype(jnp.bfloat16)
-    result = jnp.dot(updated, full, preferred_element_type=jnp.float32)
+    result = there_and_back(values, full, mix_ref[...])
     for start in range(0, slabs, group):
         at = start * lats
         parts = [result[j * rows : (j + 1) * rows, at : at + 128] for j in range(group)]
@@ -545,7 +541,7 @@
             def _(band):
                 for field in range(fields):
                     for tile in range(tiles):
-                        at = (field * tiles + tile) * count
+                        at = (field * tiles + tile) * (count + 1)
                         out_ref[field, slot, band, :, tile * 128 : (tile + 1) * 128] = held_ref[
                             base - begin + band, at : at + count, :
                         ].astype(jnp.bfloat16)
@@ -572,8 +568,8 @@
             ],
             out_specs=whole,
             scratch_shapes=[
-                pltpu.VMEM((slabs, fields * width // 128 * count, 128), jnp.float32),
-                pltpu.VMEM((rows * pairs, half), jnp.float32),
+                pltpu.VMEM((slabs, fields * width // 128 * (count + 1), 128), jnp.float32),
+                pltpu.VMEM((-(-rows * (pairs + 1) // 8) * 8, half), jnp.float32),
             ],
         ),
         out_shape=jax.ShapeDtypeStruct(arrived.shape, jnp.bfloat16),

time: 260 us -> 258 us (level)
  Pallas kernels: 213 us -> 210 us
    pallas_call x1, Pallas kernels: 48 us -> 45.4 us  [packed_transform(): pl.pallas_call(functools.partial(packed_kernel, waves, lats, spare), grid...]
where the time goes in v6:
time: 258 us; the launch traced here: 257 us
  Pallas kernels  210 us (81%)
  local copies, waits for them, and re-layouts  18.6 us (7%)
  matrix products  14.7 us (6%)
  other arithmetic  13.8 us (5%)
    pallas_call x1, Pallas kernels, outward(): pl.pallas_call(functools.partial(outward_kernel, bands), out_shape=jax.Sh...  82.6 us
    pallas_call x1, Pallas kernels, homeward(): pl.pallas_call(functools.partial(homeward_kernel, bands), out_shape=jax.S...  82 us
    pallas_call x1, Pallas kernels, packed_transform(): pl.pallas_call(functools.partial(packed_kernel, waves, lats, spare), grid...  45.4 us
    select_n x1, local copies, waits for them, and re-layouts, per_device(): return jnp.where(in_range, restored, nothing)  9.47 us
    dot_general x1, matrix products, spread_waves(): lax.dot_general(choose, flat, (((1,), (1,)), ((), ())), preferred_element...  7.86 us
    unnamed x15, local copies, waits for them, and re-layouts  6.74 us
    select_n x1, other arithmetic, per_device(): masked = jnp.where(to_spare, jnp.pad(jnp.flip(row, 3), pad), masked)  6.22 us
    dot_general x1, matrix products, gather_waves(): lax.dot_general(home, choose, (((0,), (0,)), ((), ())), preferred_element...  5.64 us

profile of v6, /device:TPU:11, one launch (start us, length us, event | category | flops | bytes accessed | tf_op | source)
XLA Modules:
  0.0 257.2 jit_solution(11924553015225875255)
XLA Ops:
  0.0 0.1 and_and_fusion
  0.1 0.7 fusion.6
  0.8 0.6 dynamic_slice.13
  1.4 0.7 slice_compare_fusion
  2.0 0.8 broadcast_select_fusion
  2.8 0.1 rev.7
  2.9 0.1 pad_bitcast_fusion.1
  3.1 0.1 iota_compare_fusion.3
  3.2 6.2 %fusion = bf16[36,32,2,1024]{3,1,0,2:T(8,128)(2,1)} fusion(bf16[36,32,2,1024]{3,2,1,0:T(2,128)(2,1)} %param.8, pred[32,1024]{1,0:T(8,128)(4,1)S(1)} %and_and_fusion, pred[32,1024]{1,0:T(8,128)(4,1)S(1)} %iota_compare_fusion.3, bf16[36,2,1024]{2,0,1:T(8,128)(2,1)S(1)} %copy.11), kind=kLoop, calls=%fused_computation.3 | loop fusion | flops 4718592 | bytes 9650176 | tf_op jit(solution)/shard_map/jit(_where)/select_n | solution.py:657
  9.4 0.1 reshape.172
  9.5 0.1 pad_add_fusion
  9.6 0.1 eq.47
  9.7 7.9 %convolution_convert_fusion.1 = bf16[1024,2304]{1,0:T(8,128)(2,1)S(1)} fusion(bf16[2304,1024]{1,0:T(8,128)(2,1)} %bitcast.35, s32[1024]{0:T(1024)S(1)} %eq.47), kind=kOutput, calls=%fused_computation.1 | convolution fusion | flops 4835246080 | bytes 9441280 | tf_op jit(solution)/shard_map/dot_general | solution.py:615
  17.5 0.0 copy-start.5
  17.5 0.0 copy-start.6
  17.5 82.6 %shard_map.82.x_ref = bf16[4,2,8,16,2304]{4,3,2,1,0:T(8,128)(2,1)S(1)} custom-call(bf16[8,4,2,16,2304]{4,3,2,1,0:T(8,128)(2,1)S(1)} %bitcast.31), custom_call_target="tpu_custom_call" | custom-call | tf_op jit(solution)/shard_map/pallas_call | solution.py:419
  100.2 2.2 copy-done.1
  102.4 0.6 dynamic_slice.12.first
  103.0 1.2 fusion.4.mix_ref
  104.2 45.4 %shard_map.83.src = bf16[4,2,8,16,2304]{4,3,2,1,0:T(8,128)(2,1)} custom-call(s32[16]{0:T(128)} %dynamic_slice.12.first, bf16[4,2,8,16,2304]{4,3,2,1,0:T(8,128)(2,1)} %copy-done.1, bf16[1025,16,128]{2,1,0:T(8,128)(2,1)} %bitcast.36, bf16[288,288]{1,0:T(8,128)(2,1)} %fusion.4.mix_ref, bf16[128,512]{1,0:T(8,128)(2,1)} %constant.61.clone.select_ref), custom_call_target="tpu_custom_call" | custom-call | flops 9975398400 | bytes 13635584 | tf_op jit(solution)/shard_map/pallas_call | solution.py:558
  149.6 2.3 copy-done.2
  151.9 82.0 %shard_map.84 = bf16[8,4,2,16,2304]{4,3,2,1,0:T(8,128)(2,1)S(1)} custom-call(bf16[4,2,8,16,2304]{4,3,2,1,0:T(8,128)(2,1)S(1)} %copy-done.2, bf16[16,2304]{1,0:T(8,128)(2,1)S(1)} %broadcast_in_dim.76.zeros), custom_call_target="tpu_custom_call" | custom-call | tf_op jit(solution)/shard_map/pallas_call | solution.py:433
  233.9 5.6 %convolution_convert_fusion = bf16[2304,1024]{1,0:T(8,128)(2,1)S(1)} fusion(bf16[1024,2304]{1,0:T(8,128)(2,1)S(1)} %bitcast.32, s32[1024]{0:T(1024)S(1)} %eq.47), kind=kOutput, calls=%fused_computation | convolution fusion | flops 4835246080 | bytes 9441280 | tf_op jit(solution)/shard_map/dot_general | solution.py:622
  239.5 0.0 copy-start.3
  239.6 2.2 copy-done.3
  241.7 0.3 dynamic-slice_bitcast_fusion
  242.1 0.1 slice.12
  242.2 0.2 rev.8
  242.4 0.1 pad_bitcast_fusion
  242.5 0.1 and_and_fusion.1
  242.6 5.1 %select_select_fusion = bf16[36,32,2,1024]{3,1,0,2:T(8,128)(2,1)} fusion(bf16[36,32,2,1024]{3,1,0,2:T(8,128)(2,1)} %bitcast.34, pred[32,1024]{1,0:T(8,128)(4,1)S(1)} %and_and_fusion.1, pred[32,1024]{1,0:T(8,128)(4,1)S(1)} %iota_compare_fusion.3, bf16[36,2,1024]{2,0,1:T(8,128)(2,1)S(1)} %copy.14), kind=kLoop, calls=%fused_computation.4 | loop fusion | flops 4718592 | bytes 9650176 | tf_op jit(solution)/shard_map/jit(_where)/select_n | solution.py:671
  247.8 9.5 %copy.15 = bf16[36,32,2,1024]{3,2,1,0:T(2,128)(2,1)} copy(bf16[36,32,2,1024]{3,1,0,2:T(8,128)(2,1)} %select_select_fusion) | data formatting | bytes 9437184 | tf_op jit(solution)/shard_map/jit(_where)/select_n | solution.py:671
  (17 shorter events, 0.1 us)
Async XLA Ops:
  0.0 103.0 %copy-start = (bf16[2,72,72]{2,1,0:T(8,128)(2,1)S(1)}, bf16[2,72,72]{2,1,0:T(8,128)(2,1)}, u32[]{:S(2)}) copy-start(bf16[2,72,72]{2,1,0:T(8,128)(2,1)} %param.12) | copy-start | bytes 62212
  3.2 6.2 %copy-start.4 = (s32[512]{0:T(512)S(1)}, s32[512]{0:T(512)}, u32[]{:S(2)}) copy-start(s32[512]{0:T(512)} %param.10) | copy-start | bytes 6148
  17.5 85.4 %copy-start.5 = (bf16[2,288,72]{1,2,0:T(8,128)(2,1)S(1)}, bf16[2,288,72]{1,2,0:T(8,128)(2,1)}, u32[]{:S(2)}) copy-start(bf16[2,288,72]{1,2,0:T(8,128)(2,1)} %constant.59.clone) | copy-start | bytes 248836
  17.5 85.4 %copy-start.6 = (pred[288,288]{1,0:T(32,128)(4,1)S(1)}, pred[288,288]{1,0:T(32,128)(4,1)}, u32[]{:S(2)}) copy-start(pred[288,288]{1,0:T(32,128)(4,1)} %constant.60.clone) | copy-start | bytes 248836
  100.2 2.2 copy-start.1
  149.5 2.3 copy-start.2
  239.5 2.2 copy-start.3
